TPU v7x, 128 devices: a whole 4x4x4 slice. The times are simulated.
128 devices in a mesh: lat: 8 (over x, core), lon: 16 (over y, z).
Axes of the slice: x: 4, y: 4, z: 4, core: 2. Of those that a mesh axis runs over, the one named last changes fastest.
Arguments:
- state: bfloat16 [8, 16, 64, 50, 8, 128], P('lat', 'lon'), may hold values from -6 to 6
- ocean_mask: int32 [8, 16, 64, 8], P('lat', 'lon'), may hold values 0 or 1
- obs_pert: bfloat16 [8, 16, 4096, 128], P('lat', 'lon'), may hold values from -20 to 20
- innovation: float32 [8, 16, 4096], P('lat', 'lon'), may hold values from -6 to 6
- precision: float32 [8, 16, 4096], P('lat', 'lon'), may hold values from 0.25 to 4
- obs_index: int32 [8, 16, 64, 256], P('lat', 'lon'), may hold values from 0 to 36863, as said below
- obs_count: int32 [8, 16, 64], P('lat', 'lon'), may hold values from 0 to 256, as said below
Outputs:
- analysis: bfloat16 [8, 16, 64, 50, 8, 128], P('lat', 'lon')
Inputs may be any that keep to these rules, and one draw needn't show every extreme that they name: `obs_index`: an entry (3 u + v) * 4096 + q names row q of the tile at latitude offset u - 1 and longitude offset v - 1 (longitudes periodic); no entry names a tile beyond the first or last row of tiles. `obs_count`: in every row of tiles exactly 512 patches have a nonzero count; the tiles of a row fall into pairs whose observed patches add up to 64, and some tile of every row has all 64 patches observed.
All inputs are finite; a program needn't handle non-finite values. No bound on the sum of `ocean_mask` on one device may be relied on, other than what follows from the above.
Results may differ from a plain program's by a relative error of at most 0.0039.
Values may be sent and summed in bfloat16 or wider, within the bound.
A program may use at most 128 MiB of HBM per device.

v0:
```python
import jax
import jax.numpy as jnp
from jax import lax
from jax.sharding import PartitionSpec as P

SWEEPS = 8


def padded_2(value, sides, width, wrap):
    for axis, dim in sides:
        devices, length = (lax.axis_size(axis), value.shape[dim])
        up = [(i, (i + 1) % devices) for i in range(devices if wrap else devices - 1)]
        down = [(j, i) for i, j in up]
        last = lax.slice_in_dim(value, length - width, length, axis=dim)
        leading = lax.slice_in_dim(value, 0, width, axis=dim)
        before = lax.ppermute(last, axis, up)
        after = lax.ppermute(leading, axis, down)
        value = jnp.concatenate([before, value, after], axis=dim)
    return value


def weights_of(picked_rows, picked_vals):
    members = picked_rows.shape[-1]
    highest = lax.Precision.HIGHEST
    gram_matrix = jnp.einsum(
        "nlk,nlj->nkj", picked_rows, picked_rows, preferred_element_type=jnp.float32
    )
    projected = jnp.einsum(
        "nlk,nl->nk", picked_rows, picked_vals, preferred_element_type=jnp.float32
    )
    identity = jnp.eye(members, dtype=jnp.float32)
    members_less = jnp.float32(members - 1)
    system = identity + gram_matrix / members_less
    frobenius = jnp.sqrt(jnp.sum(system * system, axis=(1, 2), keepdims=True))
    iterate = system / frobenius
    inverse = jnp.broadcast_to(identity, system.shape)
    for sweep in range(SWEEPS):
        update = 1.5 * identity - 0.5 * jnp.matmul(inverse, iterate, precision=highest)
        iterate = jnp.matmul(iterate, update, precision=highest)
        inverse = jnp.matmul(update, inverse, precision=highest)
    root_cov = inverse / jnp.sqrt(frobenius * members_less)
    covariance = jnp.matmul(root_cov, root_cov, precision=highest)
    mean_weight = jnp.einsum("nkj,nj->nk", covariance, projected, precision=highest)
    return (jnp.sqrt(members_less) * root_cov + mean_weight[:, :, None]).astype(jnp.bfloat16)


def analyse(columns, weights):
    values = columns.astype(jnp.float32)
    center = jnp.mean(values, axis=-1, keepdims=True)
    spread = (values - center).astype(jnp.bfloat16)
    return center + jnp.einsum(
        "nabk,nkj->nabj", spread, weights, preferred_element_type=jnp.float32
    )


def select_obs(ext_rows, ext_vals, pick_rows, in_window):
    zero_half = jnp.zeros((), jnp.bfloat16)
    picked_rows = jnp.where(in_window[..., None], ext_rows[pick_rows], zero_half)
    picked_vals = jnp.where(in_window, ext_vals[pick_rows], zero_half)
    return (picked_rows, picked_vals)


def balance(tile_loads, active, own_index, lon_count, capacity, balanced):
    patches = active.shape[0]
    active_int = active.astype(jnp.int32)
    local_rank = jnp.cumsum(active_int) - active_int
    starts = jnp.cumsum(tile_loads) - tile_loads
    peer_ids = jnp.arange(lon_count, dtype=jnp.int32)
    own_start = jnp.sum(jnp.where(peer_ids == own_index, starts, 0))
    own_load = jnp.sum(active_int)
    slot_ids = jnp.arange(capacity, dtype=jnp.int32)[None, :]
    send_order = (slot_ids * lon_count + (peer_ids[:, None] - own_start) % lon_count).reshape(-1)
    send_ok = send_order < own_load
    matches = (local_rank[None, :] == send_order[:, None]) & active[None, :]
    send_patch = jnp.sum(
        jnp.where(matches, jnp.arange(patches, dtype=jnp.int32)[None, :], 0), axis=1
    )
    run_start = jnp.clip((starts - own_index + lon_count - 1) // lon_count, 0, balanced)
    home_rank = jnp.clip(local_rank, 0, lon_count * capacity - 1)
    return (send_patch, send_ok, run_start, own_start, home_rank)


def place_runs(received, run_start, balanced):
    lon_count, capacity = (received.shape[0], received.shape[1])
    dense = jnp.zeros((balanced + capacity,) + received.shape[2:], received.dtype)

    def place_one(source, dense):
        block = lax.dynamic_index_in_dim(received, source, 0, keepdims=False)
        return lax.dynamic_update_slice_in_dim(dense, block, run_start[source], 0)

    dense = lax.fori_loop(0, lon_count, place_one, dense)
    return dense[:balanced]


def cut_runs(dense, run_start, lon_count, capacity):
    rest = dense.shape[1:]
    padded = jnp.concatenate([dense, jnp.zeros((capacity,) + rest, dense.dtype)], axis=0)
    outgoing = jnp.zeros((lon_count, capacity) + rest, dense.dtype)

    def cut_one(source, outgoing):
        block = lax.dynamic_slice_in_dim(padded, run_start[source], capacity, 0)
        return lax.dynamic_update_slice_in_dim(outgoing, block[None], source, 0)

    return lax.fori_loop(0, lon_count, cut_one, outgoing)


def home_order(arrived, own_start):
    lon_count, capacity = (arrived.shape[0], arrived.shape[1])
    turned = jnp.swapaxes(arrived, 0, 1)
    rolled = jnp.roll(turned, -own_start, axis=1)
    return rolled.reshape((lon_count * capacity,) + arrived.shape[2:])


def shards(state, ocean_mask, obs_pert, innovation, precision, obs_index, obs_count):
    members = obs_pert.shape[-1]
    pool_rows = obs_pert.shape[2]
    root_prec = jnp.sqrt(precision)
    scaled = (root_prec[..., None] * obs_pert.astype(jnp.float32)).astype(jnp.bfloat16)
    weighted = (
        (root_prec * innovation).astype(jnp.bfloat16).reshape(1, 1, pool_rows // members, members)
    )
    pool_block = jnp.concatenate([scaled, weighted], axis=2)
    lon_wide = padded_2(pool_block, (("lon", 1),), 1, True)
    neighbourhood = padded_2(lon_wide, (("lat", 0),), 1, False)
    ext_rows = neighbourhood[:, :, :pool_rows, :].reshape(9 * pool_rows, members)
    ext_vals = neighbourhood[:, :, pool_rows:, :].reshape(9 * pool_rows)
    columns = state[0, 0]
    pick_rows = obs_index[0, 0]
    counts = obs_count[0, 0]
    patches = counts.shape[0]
    obs_slots = pick_rows.shape[1]
    col_shape = columns.shape[1:]
    in_window = jnp.arange(obs_slots, dtype=jnp.int32)[None, :] < counts[:, None]
    active = counts > 0
    updated = active[:, None, None, None] & (ocean_mask[0, 0][:, None, :, None] > 0)
    zero_half = jnp.zeros((), jnp.bfloat16)
    lon_count = lax.axis_size("lon")
    capacity = -(-patches // lon_count)
    balanced = patches // 2
    tile_loads = lax.all_gather(
        jnp.sum(active.astype(jnp.int32)).reshape(1), "lon", axis=0, tiled=True
    )
    send_patch, send_ok, run_start, own_start, home_rank = balance(
        tile_loads, active, lax.axis_index("lon"), lon_count, capacity, balanced
    )
    picked_rows, picked_vals = select_obs(
        ext_rows, ext_vals, pick_rows[send_patch], in_window[send_patch] & send_ok[:, None]
    )
    moved_cols = jnp.where(send_ok[:, None, None, None], columns[send_patch], zero_half)
    got_rows, got_vals, got_cols = (
        lax.all_to_all(
            picked_rows.reshape(lon_count, capacity, obs_slots, members),
            "lon",
            split_axis=0,
            concat_axis=0,
            tiled=True,
        ),
        lax.all_to_all(
            picked_vals.reshape(lon_count, capacity, obs_slots),
            "lon",
            split_axis=0,
            concat_axis=0,
            tiled=True,
        ),
        lax.all_to_all(
            moved_cols.reshape((lon_count, capacity) + col_shape),
            "lon",
            split_axis=0,
            concat_axis=0,
            tiled=True,
        ),
    )
    dense_rows = place_runs(got_rows, run_start, balanced)
    dense_vals = place_runs(got_vals, run_start, balanced)
    dense_cols = place_runs(got_cols, run_start, balanced)
    analysed = analyse(dense_cols, weights_of(dense_rows, dense_vals)).astype(jnp.bfloat16)
    returned = cut_runs(analysed, run_start, lon_count, capacity)
    arrived = lax.all_to_all(returned, "lon", split_axis=0, concat_axis=0, tiled=True)
    analysed_home = home_order(arrived, own_start)[home_rank].astype(jnp.float32)
    result = jnp.where(updated, analysed_home, columns.astype(jnp.float32)).astype(jnp.bfloat16)
    return result[None, None]


def solution(mesh):
    placed = (
        P("lat", "lon", None, None, None, None),
        P("lat", "lon", None, None),
        P("lat", "lon", None, None),
        P("lat", "lon", None),
        P("lat", "lon", None),
        P("lat", "lon", None, None),
        P("lat", "lon", None),
    )
    return jax.shard_map(
        shards,
        mesh=mesh,
        in_specs=placed,
        out_specs=P("lat", "lon", None, None, None, None),
        check_vma=False,
    )
```

profile of v0, /device:TPU:114, one launch (start us, length us, event | category | flops | bytes accessed | tf_op | source)
XLA Modules:
  0.0 787.6 jit_solution(4816658402260522577)
XLA Ops:
  5.6 23.0 %collective-permute-done = bf16[1,1,4128,128]{3,2,1,0:T(8,128)(2,1)S(1)} collective-permute-done((bf16[1,1,4128,128]{3,2,1,0:T(8,128)(2,1)S(1)}, bf16[1,1,4128,128]{3,2,1,0:T(8,128)(2,1)S(1)}, u32[]{:S(2)}, u32[]{:S(2)}) %collective-permute-start) | collective-permute-done | bytes 1056800 | tf_op jit(solution)/shard_map/ppermute | solution.py:16
  42.6 11.2 %all-reduce.1 = s32[16]{0:T(128)S(1)} all-reduce(s32[16]{0:T(128)S(1)} %dynamic-update-slice), channel_id=1, replica_groups=mesh['lat'=8,'lon'=16] {'lon'}, use_global_device_ids=true, to_apply=%add.1 | all-reduce | flops 16 | bytes 128
  57.5 7.0 gather_fusion
  65.3 7.8 collective-permute-done.2
  75.6 100.9 %gather_fusion.4 = bf16[16384]{0:T(1024)(128)(2,1)S(1)} fusion(bf16[36864]{0:T(1024)(128)(2,1)S(1)} %bitcast.120, s32[16384]{0:T(1024)S(1)} %broadcast_clamp_fusion), kind=kCustom, calls=%fused_computation.4 | custom fusion | bytes 131072 | tf_op jit(solution)/shard_map/gather | solution.py:59
  177.3 8.0 %all-to-all-start.2 = ((bf16[16,4,256]{2,1,0:T(4,128)(2,1)}), bf16[16,4,256]{2,1,0:T(4,128)(2,1)S(1)}, u32[]{:S(2)}, u32[]{:S(2)}) async-start(bf16[16,4,256]{2,1,0:T(4,128)(2,1)} %get-tuple-element.359), calls=%async_computation.2 | async-start | bytes 65536 | tf_op jit(solution)/shard_map/all_to_all | solution.py:158
  185.3 6.1 broadcast_select_fusion
  191.4 7.2 all-to-all-start
  198.6 8.6 %pad_maximum_fusion = bf16[3,3,4128,128]{3,2,1,0:T(8,128)(2,1)} fusion(bf16[1,3,4128,128]{3,2,1,0:T(8,128)(2,1)} %collective-permute-done.3, bf16[1,1,4128,128]{3,2,1,0:T(8,128)(2,1)S(1)} %collective-permute-done.1, bf16[1,1,32,128]{3,2,1,0:T(8,128)(2,1)S(1)} %bitcast.131, bf16[1,1,4096,128]{3,2,1,0:T(8,128)(2,1)S(1)} %multiply_convert_fusion, ...), kind=kLoop, calls=%fused_computation.14 | loop fusion | flops 57065472 | bytes 19021824 | tf_op jit(solution)/shard_map/concatenate | solution.py:18
  207.2 7.9 %slice.32 = bf16[3,3,4096,128]{3,2,1,0:T(8,128)(2,1)} slice(bf16[3,3,4128,128]{3,2,1,0:T(8,128)(2,1)} %pad_maximum_fusion), slice={[0:3], [0:3], [0:4096], [0:128]} | slice | bytes 18874368 | tf_op jit(solution)/shard_map/slice | solution.py:125
  215.1 59.8 %gather_fusion.3 = bf16[16384,128]{1,0:T(8,128)(2,1)} fusion(bf16[36864,128]{1,0:T(8,128)(2,1)} %bitcast.121, s32[16384]{0:T(1024)S(1)} %broadcast_clamp_fusion), kind=kCustom, calls=%fused_computation.3 | custom fusion | bytes 8454144 | tf_op jit(solution)/shard_map/gather | solution.py:58
  274.9 7.6 broadcast_select_fusion.1
  282.5 17.0 %all-to-all-done = bf16[16,4,50,8,128]{4,3,2,1,0:T(8,128)(2,1)} async-done(((bf16[16,4,50,8,128]{4,3,2,1,0:T(8,128)(2,1)}), bf16[16,4,50,8,128]{4,3,2,1,0:T(8,128)(2,1)}, u32[]{:S(2)}, u32[]{:S(2)}) %all-to-all-start) | async-done | bytes 6553632 | tf_op jit(solution)/shard_map/all_to_all | solution.py:165
  299.5 25.0 %all-to-all-start.1 = ((bf16[16,4,256,128]{3,2,1,0:T(8,128)(2,1)}), bf16[16,4,256,128]{3,2,1,0:T(8,128)(2,1)}, u32[]{:S(2)}, u32[]{:S(2)}) async-start(bf16[16,4,256,128]{3,2,1,0:T(8,128)(2,1)} %broadcast_select_fusion.1), calls=%async_computation.1 | async-start | bytes 8388608 | tf_op jit(solution)/shard_map/all_to_all | solution.py:151
  324.6 43.2 %while.58 = (s32[]{:T(128)}, bf16[36,256]{1,0:T(8,128)(2,1)S(1)}, bf16[16,4,256]{2,1,0:T(4,128)(2,1)S(1)}, s32[16]{0:T(128)S(1)}) while((s32[]{:T(128)}, bf16[36,256]{1,0:T(8,128)(2,1)S(1)}, bf16[16,4,256]{2,1,0:T(4,128)(2,1)S(1)}, s32[16]{0:T(128)S(1)}) %tuple.121), condition=%wide.region_12.13_spmd.clone, body=%wide.region_11.12_spmd.sunk.clone | while | flops 5 | bytes 8299 | solution.py:91
  370.1 69.1 %while.56 = (s32[]{:T(128)}, bf16[36,50,8,128]{3,2,1,0:T(8,128)(2,1)}, bf16[16,4,50,8,128]{4,3,2,1,0:T(8,128)(2,1)}, s32[16]{0:T(128)S(1)}) while((s32[]{:T(128)}, bf16[36,50,8,128]{3,2,1,0:T(8,128)(2,1)}, bf16[16,4,50,8,128]{4,3,2,1,0:T(8,128)(2,1)}, s32[16]{0:T(128)S(1)}) %tuple.127), condition=%wide.region_6.7_spmd.clone, body=%wide.region_5.6_spmd.sunk.clone | while | flops 5 | bytes 819815 | solution.py:91
  443.6 55.4 %while.57 = (s32[]{:T(128)}, bf16[36,256,128]{2,1,0:T(8,128)(2,1)S(1)}, bf16[16,4,256,128]{3,2,1,0:T(8,128)(2,1)}, s32[16]{0:T(128)S(1)}) while((s32[]{:T(128)}, bf16[36,256,128]{2,1,0:T(8,128)(2,1)S(1)}, bf16[16,4,256,128]{3,2,1,0:T(8,128)(2,1)}, s32[16]{0:T(128)S(1)}) %tuple.128), condition=%wide.region_9.10_spmd.clone, body=%wide.region_8.9_spmd.sunk.clone | while | flops 5 | bytes 524395 | solution.py:91
  567.4 72.4 %while.59 = (s32[]{:T(128)}, bf16[16,4,50,8,128]{4,3,2,1,0:T(8,128)(2,1)}, s32[16]{0:T(128)S(1)}, bf16[36,50,8,128]{3,2,1,0:T(8,128)(2,1)}) while((s32[]{:T(128)}, bf16[16,4,50,8,128]{4,3,2,1,0:T(8,128)(2,1)}, s32[16]{0:T(128)S(1)}, bf16[36,50,8,128]{3,2,1,0:T(8,128)(2,1)}) %tuple.129), condition=%wide.region_14.15_spmd.clone, body=%wide.region_13.14_spmd.sunk.clone | while | flops 5 | bytes 819815 | solution.py:104
  639.8 7.4 all-to-all-start.3
  648.6 107.9 %all-to-all-done.3 = bf16[16,4,50,8,128]{4,3,2,1,0:T(8,128)(2,1)} async-done(((bf16[16,4,50,8,128]{4,3,2,1,0:T(8,128)(2,1)}), bf16[16,4,50,8,128]{4,3,2,1,0:T(8,128)(2,1)}, u32[]{:S(2)}, u32[]{:S(2)}) %all-to-all-start.3) | async-done | bytes 6553632 | tf_op jit(solution)/shard_map/all_to_all | solution.py:178
  756.4 6.1 copy.53
  762.5 7.9 %fusion.2 = bf16[4,16,50,8,128]{4,3,2,1,0:T(8,128)(2,1)} fusion(s32[]{:T(128)S(6)} %select_n.155, bf16[4,16,50,8,128]{4,3,2,1,0:T(8,128)(2,1)} %bitcast.125), kind=kLoop, calls=%fused_computation.18 | loop fusion | flops 3276800 | bytes 13107204 | tf_op jit(solution)/shard_map/jit(_roll_dynamic)/concatenate | solution.py:110
  770.4 7.0 gather_fusion.5
  777.4 9.9 %fusion = bf16[1,1,64,50,8,128]{5,4,3,2,1,0:T(8,128)(2,1)} fusion(bf16[1,1,64,50,8,128]{5,4,3,2,1,0:T(8,128)(2,1)} %param.15, bf16[64,50,8,128]{3,2,1,0:T(8,128)(2,1)} %gather_fusion.5, pred[64,8]{1,0:T(8,128)(4,1)S(1)} %copy.34), kind=kLoop, calls=%fused_computation.13 | loop fusion | flops 13107200 | bytes 19661312 | tf_op jit(solution)/shard_map/convert_element_type | solution.py:180
  (243 shorter events, 217.4 us)
Async XLA Ops:
  0.0 56.0 %copy-start = (s32[1,1,64,256]{3,2,1,0:T(8,128)S(1)}, s32[1,1,64,256]{3,2,1,0:T(8,128)}, u32[]{:S(2)}) copy-start(s32[1,1,64,256]{3,2,1,0:T(8,128)} %param.20) | copy-start | bytes 196612
  3.4 36.1 %copy-start.4 = (s32[1,1,64]{2,1,0:T(1,128)S(1)}, s32[1,1,64]{2,1,0:T(1,128)}, u32[]{:S(2)}) copy-start(s32[1,1,64]{2,1,0:T(1,128)} %param.21) | copy-start | bytes 772
  3.5 36.3 %copy-start.5 = (u32[128]{0:T(128)S(1)}, u32[128]{0:T(128)}, u32[]{:S(2)}) copy-start(u32[128]{0:T(128)} %constant.230) | copy-start | bytes 1540
  3.5 25.1 %collective-permute-start = (bf16[1,1,4128,128]{3,2,1,0:T(8,128)(2,1)S(1)}, bf16[1,1,4128,128]{3,2,1,0:T(8,128)(2,1)S(1)}, u32[]{:S(2)}, u32[]{:S(2)}) collective-permute-start(bf16[1,1,4128,128]{3,2,1,0:T(8,128)(2,1)S(1)} %pad_maximum_fusion.2), channel_id=1, source_target_pairs={{0,1},{1,2},{2,3},{3,4},{4,5},{5,6},{6,7},{7,8},{8,9},{9,10},{10,1... | collective-permute-start | bytes 3170312 | tf_op jit(solution)/shard_map/ppermute | solution.py:16
  3.5 27.3 %collective-permute-start.1 = (bf16[1,1,4128,128]{3,2,1,0:T(8,128)(2,1)S(1)}, bf16[1,1,4128,128]{3,2,1,0:T(8,128)(2,1)S(1)}, u32[]{:S(2)}, u32[]{:S(2)}) collective-permute-start(bf16[1,1,4128,128]{3,2,1,0:T(8,128)(2,1)S(1)} %pad_maximum_fusion.2), channel_id=1, source_target_pairs={{1,0},{2,1},{3,2},{4,3},{5,4},{6,5},{7,6},{8,7},{9,8},{10,9},{11,1... | collective-permute-start | bytes 3170312 | tf_op jit(solution)/shard_map/ppermute | solution.py:17
  34.0 39.2 %collective-permute-start.2 = (bf16[1,3,4128,128]{3,2,1,0:T(8,128)(2,1)}, bf16[1,3,4128,128]{3,2,1,0:T(8,128)(2,1)}, u32[]{:S(2)}, u32[]{:S(2)}) collective-permute-start(bf16[1,3,4128,128]{3,2,1,0:T(8,128)(2,1)} %pad_maximum_fusion.1), channel_id=1, source_target_pairs={{0,16},{16,32},{32,48},{48,64},{64,80},{80,96},{96,112},{1,17},{17... | collective-permute-start | bytes 9510920 | tf_op jit(solution)/shard_map/ppermute | solution.py:16
  35.9 39.0 %collective-permute-start.3 = (bf16[1,3,4128,128]{3,2,1,0:T(8,128)(2,1)}, bf16[1,3,4128,128]{3,2,1,0:T(8,128)(2,1)}, u32[]{:S(2)}, u32[]{:S(2)}) collective-permute-start(bf16[1,3,4128,128]{3,2,1,0:T(8,128)(2,1)} %pad_maximum_fusion.1), channel_id=1, source_target_pairs={{16,0},{32,16},{48,32},{64,48},{80,64},{96,80},{112,96},{17,1},{33... | collective-permute-start | bytes 9510920 | tf_op jit(solution)/shard_map/ppermute | solution.py:17
  177.3 14.1 %all-to-all-start.2 = ((bf16[16,4,256]{2,1,0:T(4,128)(2,1)}), bf16[16,4,256]{2,1,0:T(4,128)(2,1)S(1)}, u32[]{:S(2)}, u32[]{:S(2)}) async-start(bf16[16,4,256]{2,1,0:T(4,128)(2,1)} %get-tuple-element.359), calls=%async_computation.2 | async-start | bytes 65536 | tf_op jit(solution)/shard_map/all_to_all | solution.py:158
  191.4 108.2 %all-to-all-start = ((bf16[16,4,50,8,128]{4,3,2,1,0:T(8,128)(2,1)}), bf16[16,4,50,8,128]{4,3,2,1,0:T(8,128)(2,1)}, u32[]{:S(2)}, u32[]{:S(2)}) async-start(bf16[16,4,50,8,128]{4,3,2,1,0:T(8,128)(2,1)} %broadcast_select_fusion), calls=%async_computation | async-start | bytes 13107200 | tf_op jit(solution)/shard_map/all_to_all | solution.py:165
  299.5 143.5 %all-to-all-start.1 = ((bf16[16,4,256,128]{3,2,1,0:T(8,128)(2,1)}), bf16[16,4,256,128]{3,2,1,0:T(8,128)(2,1)}, u32[]{:S(2)}, u32[]{:S(2)}) async-start(bf16[16,4,256,128]{3,2,1,0:T(8,128)(2,1)} %broadcast_select_fusion.1), calls=%async_computation.1 | async-start | bytes 8388608 | tf_op jit(solution)/shard_map/all_to_all | solution.py:151
  556.7 3.7 copy-start.2
  639.8 8.6 %copy-start.3 = (s32[1,1,64,8]{2,3,1,0:T(8,128)S(1)}, s32[1,1,64,8]{2,3,1,0:T(8,128)}, u32[]{:S(2)}) copy-start(s32[1,1,64,8]{2,3,1,0:T(8,128)} %param.16) | copy-start | bytes 6148
  639.8 116.6 %all-to-all-start.3 = ((bf16[16,4,50,8,128]{4,3,2,1,0:T(8,128)(2,1)}), bf16[16,4,50,8,128]{4,3,2,1,0:T(8,128)(2,1)}, u32[]{:S(2)}, u32[]{:S(2)}) async-start(bf16[16,4,50,8,128]{4,3,2,1,0:T(8,128)(2,1)} %get-tuple-element.324), calls=%async_computation.3 | async-start | bytes 13107200 | tf_op jit(solution)/shard_map/all_to_all | solution.py:178
  777.4 9.9 %copy-start.1 = (s32[1,1,64,256]{3,2,1,0:T(8,128)S(1)}, s32[1,1,64,256]{3,2,1,0:T(8,128)}, u32[]{:S(2)}) copy-start(s32[1,1,64,256]{3,2,1,0:T(8,128)} %param.20) | copy-start | bytes 196612
where the time goes:
time: 798 us; the launch traced here: 788 us
  local copies, waits for them, and re-layouts  314 us (39%)
  waiting for transfers between devices  160 us (20%)
  loops' own time  125 us (16%)
  matrix products  66.2 us (8%)
  starting transfers between devices  55.2 us (7%)
  other arithmetic  54.9 us (7%)
  blocking collectives  11.2 us (1%)
    all_to_all x1, waiting for transfers between devices, shards(): lax.all_to_all(returned, 'lon', split_axis=0, concat_axis=0, tiled=True)  108 us
    gather x2, local copies, waits for them, and re-layouts, select_obs(): picked_vals = jnp.where(in_window, ext_vals[pick_rows], zero_half)  101 us
    another operation x3, loops' own time, place_runs(): dense = lax.fori_loop(0, lon_count, place_one, dense)  91.6 us
    gather x1, local copies, waits for them, and re-layouts, select_obs(): ext_rows[pick_rows]  59.8 us
    dynamic_update_slice x48, local copies, waits for them, and re-layouts, place_one(): return lax.dynamic_update_slice_in_dim(dense, block, run_start[source], 0)  46.8 us
    another operation x1, loops' own time, cut_runs(): return lax.fori_loop(0, lon_count, cut_one, outgoing)  33.2 us
    ppermute x2, waiting for transfers between devices, padded_2(): before = lax.ppermute(last, axis, up)  30.8 us
    dynamic_slice x48, local copies, waits for them, and re-layouts, place_one(): return lax.dynamic_update_slice_in_dim(dense, block, run_start[source], 0)  28.9 us
  transfers between devices with their start and end apart: 8, of which 6 were waited for; matrix products, arithmetic and copies ran while one was open for 20% of the time, Pallas kernels for 0%

commit v1 on v0

v1 whole, which is shorter than its diff:
```python
import functools
import jax, jax.numpy as jnp
from jax import lax
from jax.sharding import PartitionSpec as P
from jax.experimental import pallas as pl
from jax.experimental.pallas import tpu as pltpu

SWEEPS = 8
f32, bf16 = jnp.float32, jnp.bfloat16

def split(x):
    hi = x.astype(bf16)
    lo = (x - hi.astype(f32)).astype(bf16)
    return hi, lo

def wide(x):
    hi, lo = split(x)
    return jnp.concatenate([hi, lo], axis=1)

def twice(x):
    hi, lo = split(x)
    top = jnp.concatenate([hi, lo], axis=1)
    return jnp.concatenate([top, top], axis=0)

def times(left, right):
    out = jnp.dot(left, right, preferred_element_type=f32)
    half = out.shape[1] // 2
    return out[:, :half] + out[:, half:]

def body(G, CH, idx_ref, *refs):
    tiles = refs[:9]
    vals_ref, upd_ref, state_ref, out_ref, table, picked, stage, mref, zref, sem = refs[9:]
    step = pl.program_id(0)
    members = 128
    pool = tiles[0].shape[0]
    chunks = [(t, c) for t in range(9) for c in range(pool // CH)]

    @pl.when(step == 0)
    def _():
        def fetch(k):
            t, c = chunks[k]
            return pltpu.make_async_copy(tiles[t].at[pl.ds(c * CH, CH)], stage.at[k % 2], sem.at[k % 2])
        fetch(0).start()
        for k in range(len(chunks)):
            if k + 1 < len(chunks):
                fetch(k + 1).start()
            fetch(k).wait()
            t, c = chunks[k]
            base = t * pool + c * CH
            table[pl.ds(base, CH)] = stage[k % 2].astype(f32).reshape(CH, 1, members)
        table[pl.ds(9 * pool, 8)] = jnp.zeros((8, 1, members), f32)

    U = 16
    def gather(i, _):
        for u in range(U):
            r = i * U + u
            picked[pl.ds(r, 1)] = table[pl.ds(idx_ref[step * G * 256 + r], 1)]
        return 0
    lax.fori_loop(0, G * 256 // U, gather, 0)

    rows_i = lax.broadcasted_iota(jnp.int32, (members, members), 0)
    cols_i = lax.broadcasted_iota(jnp.int32, (members, members), 1)
    eye = (rows_i == cols_i).astype(f32)
    frob = []
    proj = []
    for g in range(G):
        rows = picked[pl.ds(g * 256, 256)].reshape(256, members).astype(bf16)
        gram = lax.dot_general(rows, rows, (((0,), (0,)), ((), ())), preferred_element_type=f32)
        pv = jnp.broadcast_to(vals_ref[pl.ds(step * G + g, 1), :], (8, 256)).astype(bf16)
        proj.append(jnp.dot(pv, rows, preferred_element_type=f32))
        system = eye + gram * f32(1.0 / 127.0)
        fr = jnp.sqrt(jnp.sum(system * system, axis=(0, 1), keepdims=True))
        frob.append(fr)
        A = system / fr
        W = twice(-0.5 * A)
        T = 1.5 * A + times(wide(A), W)
        mref[g] = 1.5 * T + times(wide(T), W)
        zref[g] = 1.5 * eye - 0.5 * A

    def sweep(k, _):
        for g in range(G):
            M = mref[g]
            Z = zref[g]
            W = twice(-0.5 * M)
            R = times(jnp.concatenate([wide(M), wide(Z)], axis=0), W)
            T = 1.5 * M + R[:members]
            zref[g] = 1.5 * Z + R[members:]
            mref[g] = 1.5 * T + times(wide(T), W)
        return 0
    lax.fori_loop(0, SWEEPS - 2, sweep, 0)

    for g in range(G):
        M = mref[g]
        Z = zref[g]
        Z = 1.5 * Z + times(wide(Z), twice(-0.5 * M))
        root = Z / jnp.sqrt(frob[g] * f32(127.0))
        Rw = twice(root)
        mw = times(wide(times(wide(proj[g]), Rw)), Rw)
        weights_t = (jnp.sqrt(f32(127.0)) * root + mw[:1]).astype(bf16)
        x = state_ref[g]
        values = x.astype(f32)
        center = jnp.sum(values, axis=-1, keepdims=True) * f32(1.0 / members)
        spread = (values - center).astype(bf16)
        got = center + lax.dot_general(spread, weights_t, (((1,), (1,)), ((), ())), preferred_element_type=f32)
        n = values.shape[0]
        upd = upd_ref[g]
        res = jnp.where(upd[None] > 0, got.reshape(n // 8, 8, members), values.reshape(n // 8, 8, members))
        out_ref[g] = res.reshape(n, members).astype(bf16)

def analyse_patches(idx, tiles, vals, upd, state, G=4, CH=1024):
    N = vals.shape[0]
    pool = tiles[0].shape[0]
    rows = state.shape[1]
    return pl.pallas_call(
        functools.partial(body, G, CH),
        grid_spec=pltpu.PrefetchScalarGridSpec(
            num_scalar_prefetch=1,
            grid=(N // G,),
            in_specs=[pl.BlockSpec(memory_space=pl.ANY)] * 9 + [
                pl.BlockSpec((N, 256), lambda i, s: (0, 0)),
                pl.BlockSpec((G, 8, 128), lambda i, s: (i, 0, 0)),
                pl.BlockSpec((G, rows, 128), lambda i, s: (i, 0, 0)),
            ],
            out_specs=pl.BlockSpec((G, rows, 128), lambda i, s: (i, 0, 0)),
            scratch_shapes=[
                pltpu.VMEM((9 * pool + 8, 1, 128), f32),
                pltpu.VMEM((G * 256, 1, 128), f32),
                pltpu.VMEM((2, CH, 128), bf16),
                pltpu.VMEM((G, 128, 128), f32),
                pltpu.VMEM((G, 128, 128), f32),
                pltpu.SemaphoreType.DMA((2,)),
            ],
        ),
        out_shape=jax.ShapeDtypeStruct(state.shape, bf16),
        compiler_params=pltpu.CompilerParams(vmem_limit_bytes=56 * 1024 * 1024, dimension_semantics=("arbitrary",)),
        cost_estimate=pl.CostEstimate(flops=int(64*1.2e9), bytes_accessed=24_000_000, transcendentals=0),
        name="analyse_patches",
    )(idx, *tiles, vals, upd, state)


def shift_tile(value, axis, step, wrap):
    devices = lax.axis_size(axis)
    pairs = [(i, (i + step) % devices) for i in range(devices) if wrap or 0 <= i + step < devices]
    return lax.ppermute(value, axis, pairs)


def around(value):
    row = [shift_tile(value, "lon", 1, True), value, shift_tile(value, "lon", -1, True)]
    before = [shift_tile(tile, "lat", 1, False) for tile in row]
    after = [shift_tile(tile, "lat", -1, False) for tile in row]
    return before + row + after


def shards(state, ocean_mask, obs_pert, innovation, precision, obs_index, obs_count):
    members = obs_pert.shape[-1]
    pool = obs_pert.shape[2]
    patches, slots = obs_index.shape[2:]
    root_prec = jnp.sqrt(precision[0, 0])
    scaled = (root_prec[:, None] * obs_pert[0, 0].astype(f32)).astype(bf16)
    weighted = (root_prec * innovation[0, 0]).astype(bf16).reshape(pool // members, members)
    tiles = around(scaled)
    vals = jnp.stack(around(weighted)).reshape(-1)
    counts = obs_count[0, 0]
    picks = obs_index[0, 0]
    in_window = jnp.arange(slots, dtype=jnp.int32)[None, :] < counts[:, None]
    picked_vals = jnp.where(in_window, vals[picks].astype(f32), 0.0)
    places = jnp.where(in_window, picks, 9 * pool)
    updated = ((counts > 0)[:, None] & (ocean_mask[0, 0] > 0)).astype(f32)
    updated = jnp.broadcast_to(updated[:, :, None], updated.shape + (members,))
    columns = state.reshape(patches, -1, members)
    out = analyse_patches(places.reshape(-1), tiles, picked_vals, updated, columns)
    return out.reshape(state.shape)


def solution(mesh):
    placed = (
        P("lat", "lon", None, None, None, None),
        P("lat", "lon", None, None),
        P("lat", "lon", None, None),
        P("lat", "lon", None),
        P("lat", "lon", None),
        P("lat", "lon", None, None),
        P("lat", "lon", None),
    )
    return jax.shard_map(
        shards,
        mesh=mesh,
        in_specs=placed,
        out_specs=P("lat", "lon", None, None, None, None),
        check_vma=False,
    )
```

time: 798 us -> 351 us (0.44)
  the two profiles are of different devices: /device:TPU:114 before, /device:TPU:1 now
where the time goes in v1:
time: 351 us; the launch traced here: 350 us
  Pallas kernels  186 us (53%)
  local copies, waits for them, and re-layouts  103 us (29%)
  starting transfers between devices  47.3 us (13%)
  waiting for transfers between devices  8.97 us (3%)
  other arithmetic  4.03 us (1%)
    pallas_call x1, Pallas kernels, analyse_patches(): pl.pallas_call(functools.partial(body, G, CH), grid_spec=pltpu.PrefetchSc...  186 us
    gather x1, local copies, waits for them, and re-layouts, shards(): picked_vals = jnp.where(in_window, vals[picks].astype(f32), 0.0)  101 us
    ppermute x16, starting transfers between devices, shift_tile(): return lax.ppermute(value, axis, pairs)  47.3 us
    ppermute x16, waiting for transfers between devices, shift_tile(): return lax.ppermute(value, axis, pairs)  8.97 us
  transfers between devices with their start and end apart: 16, of which 5 were waited for; matrix products, arithmetic and copies ran while one was open for 30% of the time, Pallas kernels for 0%

profile of v1, /device:TPU:1, one launch (start us, length us, event | category | flops | bytes accessed | tf_op | source)
XLA Modules:
  0.0 349.8 jit_solution(11536203169537621446)
XLA Ops:
  0.0 0.8 convert_reduce_fusion
  0.9 7.1 %collective-permute-start.11 = (bf16[32,128]{1,0:T(8,128)(2,1)S(1)}, bf16[32,128]{1,0:T(8,128)(2,1)S(1)}, u32[]{:S(2)}, u32[]{:S(2)}) collective-permute-start(bf16[32,128]{1,0:T(8,128)(2,1)S(1)} %bitcast.45), channel_id=1, source_target_pairs={{0,15},{1,0},{2,1},{3,2},{4,3},{5,4},{6,5},{7,6},{8,7},{9,8},{10,9... | collective-permute-start | bytes 24584 | tf_op jit(solution)/shard_map/ppermute | solution.py:144
  8.0 3.9 %collective-permute-start.10 = (bf16[32,128]{1,0:T(8,128)(2,1)S(1)}, bf16[32,128]{1,0:T(8,128)(2,1)S(1)}, u32[]{:S(2)}, u32[]{:S(2)}) collective-permute-start(bf16[32,128]{1,0:T(8,128)(2,1)S(1)} %bitcast.46), channel_id=1, source_target_pairs={{0,16},{16,32},{32,48},{48,64},{64,80},{80,96},{96,112},{1,17},{17... | collective-permute-start | bytes 24584 | tf_op jit(solution)/shard_map/ppermute | solution.py:144
  12.0 0.8 sqrt.20
  12.8 1.7 fusion.refs_4_
  14.5 1.9 collective-permute-start.6
  16.5 4.8 %collective-permute-start.3 = (bf16[4096,128]{1,0:T(8,128)(2,1)S(1)}, bf16[4096,128]{1,0:T(8,128)(2,1)S(1)}, u32[]{:S(2)}, u32[]{:S(2)}) collective-permute-start(bf16[4096,128]{1,0:T(8,128)(2,1)S(1)} %fusion.refs_4_), channel_id=1, source_target_pairs={{0,15},{1,0},{2,1},{3,2},{4,3},{5,4},{6,5},{7,6},{8,7},{9,8},{10,9... | collective-permute-start | bytes 3145736 | tf_op jit(solution)/shard_map/ppermute | solution.py:144
  22.2 3.9 %collective-permute-start.9 = (bf16[32,128]{1,0:T(8,128)(2,1)S(1)}, bf16[32,128]{1,0:T(8,128)(2,1)S(1)}, u32[]{:S(2)}, u32[]{:S(2)}) collective-permute-start(bf16[32,128]{1,0:T(8,128)(2,1)S(1)} %collective-permute-done.8), channel_id=1, source_target_pairs={{0,16},{16,32},{32,48},{48,64},{64,80},{80,96},{96,112},{1,17},{17... | collective-permute-start | bytes 24584 | tf_op jit(solution)/shard_map/ppermute | solution.py:144
  26.9 1.9 collective-permute-start.14
  28.8 4.2 %collective-permute-start.12 = (bf16[32,128]{1,0:T(8,128)(2,1)S(1)}, bf16[32,128]{1,0:T(8,128)(2,1)S(1)}, u32[]{:S(2)}, u32[]{:S(2)}) collective-permute-start(bf16[32,128]{1,0:T(8,128)(2,1)S(1)} %collective-permute-done.11), channel_id=1, source_target_pairs={{0,16},{16,32},{32,48},{48,64},{64,80},{80,96},{96,112},{1,17},{17... | collective-permute-start | bytes 24584 | tf_op jit(solution)/shard_map/ppermute | solution.py:144
  33.0 0.8 collective-permute-done.12
  33.8 1.9 collective-permute-start.15
  35.7 1.9 collective-permute-start.13
  37.7 2.0 collective-permute-done.15
  39.7 2.2 collective-permute-start.2
  41.9 0.9 collective-permute-done.3.refs_5_
  42.8 2.1 collective-permute-start.7
  45.0 4.6 %collective-permute-start.4 = (bf16[4096,128]{1,0:T(8,128)(2,1)S(1)}, bf16[4096,128]{1,0:T(8,128)(2,1)}, u32[]{:S(2)}, u32[]{:S(2)}) collective-permute-start(bf16[4096,128]{1,0:T(8,128)(2,1)S(1)} %collective-permute-done.3.refs_5_), channel_id=1, source_target_pairs={{0,16},{16,32},{32,48},{48,64},{64,80},{80,96},{96,112},{1,17},{17... | collective-permute-start | bytes 3145736 | tf_op jit(solution)/shard_map/ppermute | solution.py:144
  49.6 4.6 %collective-permute-done.refs_3_ = bf16[4096,128]{1,0:T(8,128)(2,1)} collective-permute-done((bf16[4096,128]{1,0:T(8,128)(2,1)S(1)}, bf16[4096,128]{1,0:T(8,128)(2,1)}, u32[]{:S(2)}, u32[]{:S(2)}) %collective-permute-start) | collective-permute-done | bytes 1048608 | tf_op jit(solution)/shard_map/ppermute | solution.py:144
  54.2 1.9 collective-permute-start.5
  56.1 4.7 %collective-permute-start.1 = (bf16[4096,128]{1,0:T(8,128)(2,1)}, bf16[4096,128]{1,0:T(8,128)(2,1)}, u32[]{:S(2)}, u32[]{:S(2)}) collective-permute-start(bf16[4096,128]{1,0:T(8,128)(2,1)} %collective-permute-done.refs_3_), channel_id=1, source_target_pairs={{0,16},{16,32},{32,48},{48,64},{64,80},{80,96},{96,112},{1,17},{17... | collective-permute-start | bytes 3145736 | tf_op jit(solution)/shard_map/ppermute | solution.py:144
  60.9 100.9 %gather_fusion = bf16[16384]{0:T(1024)(128)(2,1)S(1)} fusion(bf16[36864]{0:T(1024)(128)(2,1)S(1)} %bitcast.40, s32[16384]{0:T(1024)S(1)} %broadcast_clamp_fusion), kind=kCustom, calls=%fused_computation | custom fusion | bytes 131072 | tf_op jit(solution)/shard_map/gather | solution.py:166
  162.6 0.8 broadcast_in_dim.23.refs_10_
  163.4 186.3 %analyse_patches.1 = bf16[64,400,128]{2,1,0:T(8,128)(2,1)} custom-call(s32[16384]{0:T(1024)} %broadcast_select_fusion.1.idx_ref, bf16[4096,128]{1,0:T(8,128)(2,1)} %collective-permute-done.1.refs_0_, bf16[4096,128]{1,0:T(8,128)(2,1)} %collective-permute-done.2.refs_1_, bf16[4096,128]{1,0:T(8,128)(2,1)} %collective-permute-done.4.refs_2_, ...), custom_call_target="tpu_custom_call" | custom-call | flops 76800000000 | bytes 24000000 | tf_op jit(solution)/shard_map/analyse_patches/pallas_call | solution.py:114
  (47 shorter events, 2.5 us)
Async XLA Ops:
  0.0 21.3 %copy-start.3 = (s32[1,1,64]{2,1,0:T(1,128)S(1)}, s32[1,1,64]{2,1,0:T(1,128)}, u32[]{:S(2)}) copy-start(s32[1,1,64]{2,1,0:T(1,128)} %param.13) | copy-start | bytes 772
  0.0 21.4 %copy-start.1 = (s32[1,1,64,256]{3,2,1,0:T(8,128)S(1)}, s32[1,1,64,256]{3,2,1,0:T(8,128)}, u32[]{:S(2)}) copy-start(s32[1,1,64,256]{3,2,1,0:T(8,128)} %param.12) | copy-start | bytes 196612
  0.0 26.1 %copy-start.2 = (s32[1,1,64,8]{2,3,1,0:T(8,128)S(1)}, s32[1,1,64,8]{2,3,1,0:T(8,128)}, u32[]{:S(2)}) copy-start(s32[1,1,64,8]{2,3,1,0:T(8,128)} %param.8) | copy-start | bytes 6148
  0.9 26.0 %collective-permute-start.11 = (bf16[32,128]{1,0:T(8,128)(2,1)S(1)}, bf16[32,128]{1,0:T(8,128)(2,1)S(1)}, u32[]{:S(2)}, u32[]{:S(2)}) collective-permute-start(bf16[32,128]{1,0:T(8,128)(2,1)S(1)} %bitcast.45), channel_id=1, source_target_pairs={{0,15},{1,0},{2,1},{3,2},{4,3},{5,4},{6,5},{7,6},{8,7},{9,8},{10,9... | collective-permute-start | bytes 24584 | tf_op jit(solution)/shard_map/ppermute | solution.py:144
  8.0 20.8 %collective-permute-start.10 = (bf16[32,128]{1,0:T(8,128)(2,1)S(1)}, bf16[32,128]{1,0:T(8,128)(2,1)S(1)}, u32[]{:S(2)}, u32[]{:S(2)}) collective-permute-start(bf16[32,128]{1,0:T(8,128)(2,1)S(1)} %bitcast.46), channel_id=1, source_target_pairs={{0,16},{16,32},{32,48},{48,64},{64,80},{80,96},{96,112},{1,17},{17... | collective-permute-start | bytes 24584 | tf_op jit(solution)/shard_map/ppermute | solution.py:144
  11.9 10.3 %collective-permute-start.8 = (bf16[32,128]{1,0:T(8,128)(2,1)S(1)}, bf16[32,128]{1,0:T(8,128)(2,1)S(1)}, u32[]{:S(2)}, u32[]{:S(2)}) collective-permute-start(bf16[32,128]{1,0:T(8,128)(2,1)S(1)} %bitcast.47), channel_id=1, source_target_pairs={{0,1},{1,2},{2,3},{3,4},{4,5},{5,6},{6,7},{7,8},{8,9},{9,10},{10,1... | collective-permute-start | bytes 24584 | tf_op jit(solution)/shard_map/ppermute | solution.py:144
  14.5 147.3 %copy-start = (bf16[4096,128]{1,0:T(8,128)(2,1)}, bf16[4096,128]{1,0:T(8,128)(2,1)S(1)}, u32[]{:S(2)}) copy-start(bf16[4096,128]{1,0:T(8,128)(2,1)S(1)} %fusion.refs_4_) | copy-start | bytes 3145732
  14.5 41.6 %collective-permute-start.6 = (bf16[4096,128]{1,0:T(8,128)(2,1)S(1)}, bf16[4096,128]{1,0:T(8,128)(2,1)S(1)}, u32[]{:S(2)}, u32[]{:S(2)}) collective-permute-start(bf16[4096,128]{1,0:T(8,128)(2,1)S(1)} %fusion.refs_4_), channel_id=1, source_target_pairs={{16,0},{32,16},{48,32},{64,48},{80,64},{96,80},{112,96},{17,1},{33... | collective-permute-start | bytes 3145736 | tf_op jit(solution)/shard_map/ppermute | solution.py:144
  16.5 26.4 %collective-permute-start.3 = (bf16[4096,128]{1,0:T(8,128)(2,1)S(1)}, bf16[4096,128]{1,0:T(8,128)(2,1)S(1)}, u32[]{:S(2)}, u32[]{:S(2)}) collective-permute-start(bf16[4096,128]{1,0:T(8,128)(2,1)S(1)} %fusion.refs_4_), channel_id=1, source_target_pairs={{0,15},{1,0},{2,1},{3,2},{4,3},{5,4},{6,5},{7,6},{8,7},{9,8},{10,9... | collective-permute-start | bytes 3145736 | tf_op jit(solution)/shard_map/ppermute | solution.py:144
  22.2 4.7 %collective-permute-start.9 = (bf16[32,128]{1,0:T(8,128)(2,1)S(1)}, bf16[32,128]{1,0:T(8,128)(2,1)S(1)}, u32[]{:S(2)}, u32[]{:S(2)}) collective-permute-start(bf16[32,128]{1,0:T(8,128)(2,1)S(1)} %collective-permute-done.8), channel_id=1, source_target_pairs={{0,16},{16,32},{32,48},{48,64},{64,80},{80,96},{96,112},{1,17},{17... | collective-permute-start | bytes 24584 | tf_op jit(solution)/shard_map/ppermute | solution.py:144
  26.9 27.3 %collective-permute-start = (bf16[4096,128]{1,0:T(8,128)(2,1)S(1)}, bf16[4096,128]{1,0:T(8,128)(2,1)}, u32[]{:S(2)}, u32[]{:S(2)}) collective-permute-start(bf16[4096,128]{1,0:T(8,128)(2,1)S(1)} %fusion.refs_4_), channel_id=1, source_target_pairs={{0,1},{1,2},{2,3},{3,4},{4,5},{5,6},{6,7},{7,8},{8,9},{9,10},{10,1... | collective-permute-start | bytes 3145736 | tf_op jit(solution)/shard_map/ppermute | solution.py:144
  26.9 8.9 %collective-permute-start.14 = (bf16[32,128]{1,0:T(8,128)(2,1)S(1)}, bf16[32,128]{1,0:T(8,128)(2,1)S(1)}, u32[]{:S(2)}, u32[]{:S(2)}) collective-permute-start(bf16[32,128]{1,0:T(8,128)(2,1)S(1)} %bitcast.48), channel_id=1, source_target_pairs={{16,0},{32,16},{48,32},{64,48},{80,64},{96,80},{112,96},{17,1},{33... | collective-permute-start | bytes 24584 | tf_op jit(solution)/shard_map/ppermute | solution.py:144
  28.8 5.0 %collective-permute-start.12 = (bf16[32,128]{1,0:T(8,128)(2,1)S(1)}, bf16[32,128]{1,0:T(8,128)(2,1)S(1)}, u32[]{:S(2)}, u32[]{:S(2)}) collective-permute-start(bf16[32,128]{1,0:T(8,128)(2,1)S(1)} %collective-permute-done.11), channel_id=1, source_target_pairs={{0,16},{16,32},{32,48},{48,64},{64,80},{80,96},{96,112},{1,17},{17... | collective-permute-start | bytes 24584 | tf_op jit(solution)/shard_map/ppermute | solution.py:144
  33.8 5.9 %collective-permute-start.15 = (bf16[32,128]{1,0:T(8,128)(2,1)S(1)}, bf16[32,128]{1,0:T(8,128)(2,1)S(1)}, u32[]{:S(2)}, u32[]{:S(2)}) collective-permute-start(bf16[32,128]{1,0:T(8,128)(2,1)S(1)} %collective-permute-done.11), channel_id=1, source_target_pairs={{16,0},{32,16},{48,32},{64,48},{80,64},{96,80},{112,96},{17,1},{33... | collective-permute-start | bytes 24584 | tf_op jit(solution)/shard_map/ppermute | solution.py:144
  35.7 9.3 %collective-permute-start.13 = (bf16[32,128]{1,0:T(8,128)(2,1)S(1)}, bf16[32,128]{1,0:T(8,128)(2,1)S(1)}, u32[]{:S(2)}, u32[]{:S(2)}) collective-permute-start(bf16[32,128]{1,0:T(8,128)(2,1)S(1)} %collective-permute-done.8), channel_id=1, source_target_pairs={{16,0},{32,16},{48,32},{64,48},{80,64},{96,80},{112,96},{17,1},{33... | collective-permute-start | bytes 24584 | tf_op jit(solution)/shard_map/ppermute | solution.py:144
  39.7 122.8 %collective-permute-start.2 = (bf16[4096,128]{1,0:T(8,128)(2,1)S(1)}, bf16[4096,128]{1,0:T(8,128)(2,1)}, u32[]{:S(2)}, u32[]{:S(2)}) collective-permute-start(bf16[4096,128]{1,0:T(8,128)(2,1)S(1)} %fusion.refs_4_), channel_id=1, source_target_pairs={{0,16},{16,32},{32,48},{48,64},{64,80},{80,96},{96,112},{1,17},{17... | collective-permute-start | bytes 3145736 | tf_op jit(solution)/shard_map/ppermute | solution.py:144
  42.8 119.0 %copy-start.5 = (bf16[4096,128]{1,0:T(8,128)(2,1)}, bf16[4096,128]{1,0:T(8,128)(2,1)S(1)}, u32[]{:S(2)}) copy-start(bf16[4096,128]{1,0:T(8,128)(2,1)S(1)} %collective-permute-done.3.refs_5_) | copy-start | bytes 3145732
  42.8 119.7 %collective-permute-start.7 = (bf16[4096,128]{1,0:T(8,128)(2,1)S(1)}, bf16[4096,128]{1,0:T(8,128)(2,1)}, u32[]{:S(2)}, u32[]{:S(2)}) collective-permute-start(bf16[4096,128]{1,0:T(8,128)(2,1)S(1)} %collective-permute-done.3.refs_5_), channel_id=1, source_target_pairs={{16,0},{32,16},{48,32},{64,48},{80,64},{96,80},{112,96},{17,1},{33... | collective-permute-start | bytes 3145736 | tf_op jit(solution)/shard_map/ppermute | solution.py:144
  45.0 117.5 %collective-permute-start.4 = (bf16[4096,128]{1,0:T(8,128)(2,1)S(1)}, bf16[4096,128]{1,0:T(8,128)(2,1)}, u32[]{:S(2)}, u32[]{:S(2)}) collective-permute-start(bf16[4096,128]{1,0:T(8,128)(2,1)S(1)} %collective-permute-done.3.refs_5_), channel_id=1, source_target_pairs={{0,16},{16,32},{32,48},{48,64},{64,80},{80,96},{96,112},{1,17},{17... | collective-permute-start | bytes 3145736 | tf_op jit(solution)/shard_map/ppermute | solution.py:144
  54.2 108.4 %collective-permute-start.5 = (bf16[4096,128]{1,0:T(8,128)(2,1)}, bf16[4096,128]{1,0:T(8,128)(2,1)}, u32[]{:S(2)}, u32[]{:S(2)}) collective-permute-start(bf16[4096,128]{1,0:T(8,128)(2,1)} %collective-permute-done.refs_3_), channel_id=1, source_target_pairs={{16,0},{32,16},{48,32},{64,48},{80,64},{96,80},{112,96},{17,1},{33... | collective-permute-start | bytes 3145736 | tf_op jit(solution)/shard_map/ppermute | solution.py:144
  56.1 105.7 %copy-start.4 = (bf16[4096,128]{1,0:T(8,128)(2,1)}, bf16[4096,128]{1,0:T(8,128)(2,1)S(1)}, u32[]{:S(2)}) copy-start(bf16[4096,128]{1,0:T(8,128)(2,1)S(1)} %collective-permute-done.6.refs_7_) | copy-start | bytes 3145732
  56.1 106.5 %collective-permute-start.1 = (bf16[4096,128]{1,0:T(8,128)(2,1)}, bf16[4096,128]{1,0:T(8,128)(2,1)}, u32[]{:S(2)}, u32[]{:S(2)}) collective-permute-start(bf16[4096,128]{1,0:T(8,128)(2,1)} %collective-permute-done.refs_3_), channel_id=1, source_target_pairs={{0,16},{16,32},{32,48},{48,64},{64,80},{80,96},{96,112},{1,17},{17... | collective-permute-start | bytes 3145736 | tf_op jit(solution)/shard_map/ppermute | solution.py:144

commit v2 on v1

v2 whole, which is shorter than its diff:
```python
import functools
import jax, jax.numpy as jnp
from jax import lax
from jax.sharding import PartitionSpec as P
from jax.experimental import pallas as pl
from jax.experimental.pallas import tpu as pltpu

SWEEPS = 8
f32, bf16 = jnp.float32, jnp.bfloat16

def wide(x):
    hi = x.astype(bf16)
    lo = (x - hi.astype(f32)).astype(bf16)
    return jnp.concatenate([hi, lo], axis=1)

def times(left, right):
    out = jnp.dot(left, jnp.concatenate([right, right], axis=0), preferred_element_type=f32)
    half = out.shape[1] // 2
    return out[:, :half] + out[:, half:]

def body(G, CH, AB, idx_ref, val_ref, *refs):
    tiles = refs[:9]
    upd_ref, state_ref, out_ref, table, picked, stage, acc, nref, tref, zref, wref, sem = refs[9:]
    step = pl.program_id(0)
    steps = pl.num_programs(0)
    members = 128
    lanes = idx_ref.shape[1]
    slots = picked.shape[1] // G
    per = slots // lanes
    pool = tiles[0].shape[0]
    inner = SWEEPS - 2

    def pick(group, buf, g, start, count):
        p = (group * G + g) * per
        base = pl.multiple_of(g * slots, slots)
        sums = [jnp.zeros((1, members), f32) for _ in range(4)]
        for u in range(start, start + count):
            i = idx_ref[p + u // lanes, u % lanes]
            row = table[pl.ds(i, 1), :]
            picked[buf, pl.ds(base + u, 1), :] = row
            sums[u % 4] = sums[u % 4] + row * val_ref[i]
        return (sums[0] + sums[1]) + (sums[2] + sums[3])

    def fetch(t):
        return pltpu.make_async_copy(tiles[t].at[pl.ds(0, pool)], stage.at[t], sem.at[t])

    @pl.when(step == (-1 if 't' in AB else 0))
    def _():
        for t in range(9):
            fetch(t).start()
        for t in range(9):
            fetch(t).wait()
            def convert(c, _):
                table[pl.ds(t * pool + c * CH, CH), :] = stage[t, pl.ds(c * CH, CH), :].astype(f32)
                return 0
            lax.fori_loop(0, pool // CH, convert, 0)
        table[pl.ds(9 * pool, 8)] = jnp.zeros((8, members), f32)

    @pl.when(step == 0)
    def _():
        def first(g, _):
            acc[0, g] = jnp.broadcast_to(pick(0, 0, g, 0, slots), (8, members))
            return 0
        lax.fori_loop(0, G, first, 0)

    now = lax.rem(step, 2)
    nxt = 1 - now
    group = jnp.minimum(step + 1, steps - 1)

    rows_i = lax.broadcasted_iota(jnp.int32, (members, members), 0)
    cols_i = lax.broadcasted_iota(jnp.int32, (members, members), 1)
    eye = (rows_i == cols_i).astype(f32)
    frob = []
    for g in range(G):
        rows = picked[now, pl.ds(g * slots, slots), :].astype(bf16)
        gram = lax.dot_general(rows, rows, (((0,), (0,)), ((), ())), preferred_element_type=f32)
        system = eye + gram * f32(1.0 / 127.0)
        fr = jnp.sqrt(jnp.sum(system * system, axis=(0, 1), keepdims=True))
        frob.append(fr)
        n = system * (-0.5 / fr)
        nref[g] = n
        zref[g] = 1.5 * eye + n
        wref[g] = wide(n)
    for g in range(G):
        nw = wref[g]
        tref[g] = 1.5 * nref[g] + times(nw, nw)
    for g in range(inner, G):
        acc[nxt, g] = jnp.broadcast_to(pick(group, nxt, g, 0, slots), (8, members))
    for g in range(G):
        t = tref[g]
        nref[g] = 1.5 * t + times(wide(t), wref[g])

    def sweep(k, _):
        total = jnp.zeros((1, members), f32)
        for g in range(G):
            n = nref[g]
            z = zref[g]
            nw = wide(n)
            wref[g] = nw
            R = times(jnp.concatenate([nw, wide(z)], axis=0), nw)
            tref[g] = 1.5 * n + R[:members]
            zref[g] = 1.5 * z + R[members:]
            if 'g' not in AB:
                total = total + pick(group, nxt, k, g * (slots // G), slots // G)
        acc[nxt, k] = jnp.broadcast_to(total, (8, members))
        for g in range(G):
            t = tref[g]
            nref[g] = 1.5 * t + times(wide(t), wref[g])
        return 0
    lax.fori_loop(0, 0 if 's' in AB else inner, sweep, 0)

    if 'e' not in AB:
      for g in range(G):
        z = zref[g]
        z = 1.5 * z + times(wide(z), wide(nref[g]))
        root = z / jnp.sqrt(frob[g] * f32(127.0))
        zref[g] = root
        wref[g] = wide(root)
      means = []
      for g in range(G):
        proj = acc[now, g]
        means.append(times(wide(proj), wref[g]))
      for g in range(G):
        means[g] = times(wide(means[g]), wref[g])
      for g in range(G):
        weights_t = (jnp.sqrt(f32(127.0)) * zref[g] + means[g][:1]).astype(bf16)
        values = state_ref[g].astype(f32)
        center = jnp.sum(values, axis=-1, keepdims=True) * f32(1.0 / members)
        spread = (values - center).astype(bf16)
        got = center + lax.dot_general(spread, weights_t, (((1,), (1,)), ((), ())), preferred_element_type=f32)
        n = values.shape[0]
        res = jnp.where(upd_ref[g][None] > 0, got.reshape(n // 8, 8, members), values.reshape(n // 8, 8, members))
        out_ref[g] = res.reshape(n, members).astype(bf16)

def analyse_patches(idx, vals, tiles, upd, state, G=8, CH=512, AB=''):
    N = state.shape[0]
    slots = idx.size // N
    idx = idx.reshape(-1, 128)
    pool = tiles[0].shape[0]
    rows = state.shape[1]
    return pl.pallas_call(
        functools.partial(body, G, CH, AB),
        grid_spec=pltpu.PrefetchScalarGridSpec(
            num_scalar_prefetch=2,
            grid=(N // G,),
            in_specs=[pl.BlockSpec(memory_space=pl.ANY)] * 9 + [
                pl.BlockSpec((G, 8, 128), lambda i, *s: (i, 0, 0)),
                pl.BlockSpec((G, rows, 128), lambda i, *s: (i, 0, 0)),
            ],
            out_specs=pl.BlockSpec((G, rows, 128), lambda i, *s: (i, 0, 0)),
            scratch_shapes=[
                pltpu.VMEM((9 * pool + 8, 128), f32),
                pltpu.VMEM((2, G * slots, 128), f32),
                pltpu.VMEM((9, pool, 128), bf16),
                pltpu.VMEM((2, G, 8, 128), f32),
                pltpu.VMEM((G, 128, 128), f32),
                pltpu.VMEM((G, 128, 128), f32),
                pltpu.VMEM((G, 128, 128), f32),
                pltpu.VMEM((G, 128, 256), bf16),
                pltpu.SemaphoreType.DMA((9,)),
            ],
        ),
        out_shape=jax.ShapeDtypeStruct(state.shape, bf16),
        compiler_params=pltpu.CompilerParams(vmem_limit_bytes=56 * 1024 * 1024, dimension_semantics=("arbitrary",)),
        cost_estimate=pl.CostEstimate(flops=int(64*1.2e9), bytes_accessed=24_000_000, transcendentals=0),
        name="analyse_patches",
    )(idx, vals, *tiles, upd, state)


MESH = pl.DeviceIdType.MESH
PIECES = 4


def halo_body(lats, lons, own, own_vals, zeros, *refs):
    outs = refs[:8]
    vals = refs[8]
    row_send, row_recv, val_send, val_recv, local = refs[9:]
    a, b = lax.axis_index("lat"), lax.axis_index("lon")
    pool = own.shape[0]
    size = pool // PIECES
    slots = {}
    for u in range(3):
        for v in range(3):
            if (u, v) != (1, 1):
                slots[u, v] = outs[len(slots)]

    def at(u, v):
        return (a + u, lax.rem(b + v + lons, lons))

    def rows(u, v, source, target, piece, number):
        return pltpu.make_async_remote_copy(
            src_ref=source.at[pl.ds(piece * size, size)],
            dst_ref=slots[target].at[pl.ds(piece * size, size)],
            send_sem=row_send.at[number, piece],
            recv_sem=row_recv.at[number, piece],
            device_id=at(u, v),
            device_id_type=MESH,
        )

    def place(u, v):
        return vals.at[pl.ds((3 * u + v) * pool, pool)]

    def numbers(u, v, source, target, number):
        return pltpu.make_async_remote_copy(
            src_ref=source,
            dst_ref=place(*target),
            send_sem=val_send.at[number],
            recv_sem=val_recv.at[number],
            device_id=at(u, v),
            device_id_type=MESH,
        )

    has_up, has_down = a > 0, a < lats - 1
    barrier = pltpu.get_barrier_semaphore()
    for v in (-1, 1):
        pl.semaphore_signal(barrier, inc=1, device_id=at(0, v), device_id_type=MESH)

    @pl.when(has_up)
    def _():
        pl.semaphore_signal(barrier, inc=1, device_id=at(-1, 0), device_id_type=MESH)

    @pl.when(has_down)
    def _():
        pl.semaphore_signal(barrier, inc=1, device_id=at(1, 0), device_id_type=MESH)

    pl.semaphore_wait(barrier, 2 + jnp.minimum(a, 1) + jnp.minimum(lats - 1 - a, 1))

    keep = [
        pltpu.make_async_copy(own_vals, place(1, 1), local.at[0]),
        pltpu.make_async_copy(zeros, vals.at[pl.ds(9 * pool, zeros.shape[0])], local.at[1]),
    ]
    for copy in keep:
        copy.start()

    sides = [(0, 1), (0, -1)]
    across = [rows(0, 1, own, (1, 0), p, 0) for p in range(PIECES)], [rows(0, -1, own, (1, 2), p, 1) for p in range(PIECES)]
    across_vals = [numbers(0, 1, own_vals, (1, 0), 0), numbers(0, -1, own_vals, (1, 2), 1)]
    source = [slots[1, 0], own, slots[1, 2]]
    source_vals = [place(1, 0), own_vals, place(1, 2)]
    down = [[rows(1, 0, source[w], (0, w), p, 2 + 2 * w) for p in range(PIECES)] for w in range(3)]
    up = [[rows(-1, 0, source[w], (2, w), p, 3 + 2 * w) for p in range(PIECES)] for w in range(3)]
    down_vals = [numbers(1, 0, source_vals[w], (0, w), 2 + 2 * w) for w in range(3)]
    up_vals = [numbers(-1, 0, source_vals[w], (2, w), 3 + 2 * w) for w in range(3)]

    for copy in across_vals:
        copy.start()
    for p in range(PIECES):
        across[0][p].start()
        across[1][p].start()

    def onward(copies_down, copies_up):
        @pl.when(has_down)
        def _():
            for copy in copies_down:
                copy.start()

        @pl.when(has_up)
        def _():
            for copy in copies_up:
                copy.start()

    onward([down_vals[1]] + down[1], [up_vals[1]] + up[1])
    across_vals[0].wait_recv()
    onward([down_vals[0]], [up_vals[0]])
    across_vals[1].wait_recv()
    onward([down_vals[2]], [up_vals[2]])
    for p in range(PIECES):
        for d in range(2):
            across[d][p].wait_recv()
            onward([down[2 * d][p]], [up[2 * d][p]])

    for copy in keep:
        copy.wait()
    for copy in across_vals + across[0] + across[1]:
        copy.wait_send()

    @pl.when(has_down)
    def _():
        for copy in down_vals + sum(down, []):
            copy.wait_send()
        for copy in up_vals + sum(up, []):
            copy.wait_recv()

    @pl.when(has_up)
    def _():
        for copy in up_vals + sum(up, []):
            copy.wait_send()
        for copy in down_vals + sum(down, []):
            copy.wait_recv()


def halo(own, own_vals):
    lats, lons = lax.axis_size("lat"), lax.axis_size("lon")
    pool, members = own.shape
    tail = jnp.zeros((1024,), f32)
    got = pl.pallas_call(
        functools.partial(halo_body, lats, lons),
        in_specs=[pl.BlockSpec(memory_space=pl.ANY)] * 3,
        out_specs=[pl.BlockSpec(memory_space=pl.ANY)] * 9,
        out_shape=[jax.ShapeDtypeStruct((pool, members), bf16)] * 8
        + [jax.ShapeDtypeStruct((9 * pool + 1024,), f32)],
        scratch_shapes=[
            pltpu.SemaphoreType.DMA((8, PIECES)),
            pltpu.SemaphoreType.DMA((8, PIECES)),
            pltpu.SemaphoreType.DMA((8,)),
            pltpu.SemaphoreType.DMA((8,)),
            pltpu.SemaphoreType.DMA((2,)),
        ],
        compiler_params=pltpu.CompilerParams(collective_id=0, has_side_effects=True),
        name="halo",
    )(own, own_vals, tail)
    return list(got[:4]) + [own] + list(got[4:8]), got[8]


def shards(state, ocean_mask, obs_pert, innovation, precision, obs_index, obs_count):
    members = obs_pert.shape[-1]
    pool = obs_pert.shape[2]
    patches, slots = obs_index.shape[2:]
    root_prec = jnp.sqrt(precision[0, 0])
    scaled = (root_prec[:, None] * obs_pert[0, 0].astype(f32)).astype(bf16)
    weighted = (root_prec * innovation[0, 0]).astype(bf16).astype(f32)
    tiles, vals = halo(scaled, weighted)
    counts = obs_count[0, 0]
    picks = obs_index[0, 0]
    in_window = jnp.arange(slots, dtype=jnp.int32)[None, :] < counts[:, None]
    places = jnp.where(in_window, picks, 9 * pool)
    updated = ((counts > 0)[:, None] & (ocean_mask[0, 0] > 0)).astype(f32)
    updated = jnp.broadcast_to(updated[:, :, None], updated.shape + (members,))
    columns = state.reshape(patches, -1, members)
    out = analyse_patches(places, vals, tiles, updated, columns)
    return out.reshape(state.shape)


def solution(mesh):
    placed = (
        P("lat", "lon", None, None, None, None),
        P("lat", "lon", None, None),
        P("lat", "lon", None, None),
        P("lat", "lon", None),
        P("lat", "lon", None),
        P("lat", "lon", None, None),
        P("lat", "lon", None),
    )
    return jax.shard_map(
        shards,
        mesh=mesh,
        in_specs=placed,
        out_specs=P("lat", "lon", None, None, None, None),
        check_vma=False,
    )
```

time: 351 us -> 120 us (0.34)
  local copies, waits for them, and re-layouts: 103 us -> 4 us
  Pallas kernels: 186 us -> 110 us
  starting transfers between devices: 47.3 us -> 0 us
  waiting for transfers between devices: 8.97 us -> 0 us
    gather x1 -> x0, local copies, waits for them, and re-layouts: 101 us -> none  [shards(): picked_vals = jnp.where(in_window, vals[picks].astype(f32), 0.0)]
    pallas_call x1 -> x2, Pallas kernels: 186 us -> 110 us  [the longest x1 64 us: analyse_patches(): pl.pallas_call(functools.partial(body, G, CH, AB), grid_spec=pltpu.Prefet...]
    ppermute x16 -> x0, starting transfers between devices: 47.3 us -> none  [shift_tile(): return lax.ppermute(value, axis, pairs)]
    ppermute x16 -> x0, waiting for transfers between devices: 8.97 us -> none  [shift_tile(): return lax.ppermute(value, axis, pairs)]
  transfers between devices with their start and end apart: 16 -> 0, of which waited for: 5 -> 0; matrix products, arithmetic and copies ran while one was open for 30% -> 0% of each run, Pallas kernels for 0% -> 0%
where the time goes in v2:
time: 120 us
  Pallas kernels  110 us (92%)
  other arithmetic  5.94 us (5%)
  local copies, waits for them, and re-layouts  4 us (3%)
    pallas_call x1, Pallas kernels, analyse_patches(): pl.pallas_call(functools.partial(body, G, CH, AB), grid_spec=pltpu.Prefet...  64 us
    pallas_call x1, Pallas kernels, halo(): pl.pallas_call(functools.partial(halo_body, lats, lons), in_specs=[pl.Blo...  45.8 us
    convert_element_type x1, other arithmetic, shards(): scaled = (root_prec[:, None] * obs_pert[0, 0].astype(f32)).astype(bf16)  2.54 us

profile of v2, /device:TPU:1, one launch (start us, length us, event | category | flops | bytes accessed | tf_op | source)
XLA Modules:
  0.0 119.7 jit_solution(4828821192289882462)
XLA Ops:
  0.0 0.7 broadcast_compare_fusion
  0.7 0.7 fusion.2
  1.4 0.8 sqrt.10
  2.1 1.3 %fusion.1.own_vals = f32[4096]{0:T(1024)} fusion(f32[4096]{0:T(1024)S(1)} %bitcast.17, f32[4096]{0:T(1024)} %bitcast.19), kind=kLoop, calls=%fused_computation.4 | loop fusion | flops 12288 | bytes 49152 | tf_op jit(solution)/shard_map/convert_element_type | solution.py:321
  3.4 0.1 copy.9
  3.5 0.7 lt.34
  4.3 0.1 lt.35
  4.4 0.8 squeeze.4
  5.3 0.7 compare_select_fusion.idx_ref
  6.0 0.8 broadcast_in_dim.18.refs_9_
  6.8 2.5 %fusion.own.refs_4_ = bf16[4096,128]{1,0:T(8,128)(2,1)} fusion(bf16[1,1,4096,128]{3,2,1,0:T(8,128)(2,1)} %param.9, f32[4096]{0:T(1024)S(1)} %bitcast.18), kind=kLoop, calls=%fused_computation.1 | loop fusion | flops 1572864 | bytes 2113536 | tf_op jit(solution)/shard_map/convert_element_type | solution.py:320
  9.4 0.6 broadcast_in_dim.9.zeros
  10.0 45.8 %halo.1 = (bf16[4096,128]{1,0:T(8,128)(2,1)}, bf16[4096,128]{1,0:T(8,128)(2,1)}, bf16[4096,128]{1,0:T(8,128)(2,1)}, bf16[4096,128]{1,0:T(8,128)(2,1)}, bf16[4096...) custom-call(bf16[4096,128]{1,0:T(8,128)(2,1)} %fusion.own.refs_4_, ...), custom_call_target="tpu_custom_call" | custom-call | tf_op jit(solution)/shard_map/halo/pallas_call | solution.py:296
  55.7 64.0 %analyse_patches.1 = bf16[64,400,128]{2,1,0:T(8,128)(2,1)} custom-call(s32[128,128]{1,0:T(8,128)} %compare_select_fusion.idx_ref, f32[37888]{0:T(1024)} %get-tuple-element.14.val_ref, bf16[4096,128]{1,0:T(8,128)(2,1)} %get-tuple-element.15.refs_0_, bf16[4096,128]{1,0:T(8,128)(2,1)} %get-tuple-element.16.refs_1_, ...), custom_call_target="tpu_custom_call" | custom-call | flops 76800000000 | bytes 24000000 | tf_op jit(solution)/shard_map/analyse_patches/pallas_call | solution.py:141
  (2 shorter events, 0.0 us)

commit v3 on v2

v3 whole, which is shorter than its diff:
```python
import functools
import jax, jax.numpy as jnp
from jax import lax
from jax.sharding import PartitionSpec as P
from jax.experimental import pallas as pl
from jax.experimental.pallas import tpu as pltpu

SWEEPS = 8
f32, bf16 = jnp.float32, jnp.bfloat16
ROOT = 4.6128878647175444
SLOPE_A, SHIFT_A = (3 + ROOT) / 2, 3 * ROOT / 4
SLOPE_B, SHIFT_B = (6 - ROOT) / 2, 3 / ROOT

def wide(x):
    hi = x.astype(bf16)
    lo = (x - hi.astype(f32)).astype(bf16)
    return jnp.concatenate([hi, lo], axis=1)

def times(left, right):
    out = jnp.dot(left, jnp.concatenate([right, right], axis=0), preferred_element_type=f32)
    half = out.shape[1] // 2
    return out[:, :half] + out[:, half:]

def body(G, CH, AB, count_ref, mask_ref, idx_hbm, val_hbm, *refs):
    tiles = refs[:9]
    state_ref, out_ref, idx_ref, val_ref, table, picked, worth, diag, stage, acc, mref, tref, zref, wref, qref, sem, smem_sem = refs[9:]
    step = pl.program_id(0)
    steps = pl.num_programs(0)
    members = 128
    lanes = idx_ref.shape[1]
    slots = picked.shape[0] // G
    patches = steps * G
    pool = tiles[0].shape[0]

    def pick(group, g, start, count):
        p = group * G + g
        base = pl.multiple_of(g * slots, slots)
        for u in range(start, start + count):
            i = idx_ref[p + u // lanes * patches, u % lanes]
            picked[pl.ds(base + u, 1), :] = table[pl.ds(i, 1), :]
            worth[pl.ds(base + u, 1), :] = jnp.full((1, members), val_ref[i], f32)

    rows_i = lax.broadcasted_iota(jnp.int32, (members, members), 0)
    cols_i = lax.broadcasted_iota(jnp.int32, (members, members), 1)
    eye = (rows_i == cols_i).astype(f32)

    def fetch(t):
        return pltpu.make_async_copy(tiles[t].at[pl.ds(0, pool)], stage.at[t], sem.at[t])

    @pl.when(step == (-1 if 't' in AB else 0))
    def _():
        scalars = [pltpu.make_async_copy(idx_hbm, idx_ref, smem_sem.at[0]), pltpu.make_async_copy(val_hbm, val_ref, smem_sem.at[1])]
        for copy in scalars:
            copy.start()
        for t in range(9):
            fetch(t).start()
        for t in range(9):
            fetch(t).wait()
            def convert(c, _):
                table[pl.ds(t * pool + c * CH, CH), :] = stage[t, pl.ds(c * CH, CH), :].astype(f32)
                return 0
            lax.fori_loop(0, pool // CH, convert, 0)
        table[pl.ds(9 * pool, 8)] = jnp.zeros((8, members), f32)
        for copy in scalars:
            copy.wait()

    @pl.when(step == 0)
    def _():
        for j in range(2):
            diag[j] = eye * (SHIFT_A, SHIFT_B)[j]

        def first(g, _):
            pick(0, g, 0, slots)
            return 0
        lax.fori_loop(0, G, first, 0)

    group = jnp.minimum(step + 1, steps - 1)

    column = lax.broadcasted_iota(jnp.int32, (8, members), 0)

    def gather(patches, stage_no):
        count = len(patches) * slots // 4 // G
        def some(g):
            for u in range((stage_no * G + g) * count, (stage_no * G + g + 1) * count, 8):
                pick(group, patches[u // slots], u % slots, 8)
        return some

    def nothing(g):
        pass

    def square(some):
        for g in range(G):
            mw = wide(mref[g])
            wref[g] = mw
            tref[g] = times(mw, mw)
            some(g)

    def factor(some):
        for g in range(G):
            m, m2 = mref[g], tref[g]
            left = m2 - SLOPE_A * m + diag[0]
            right = m2 - SLOPE_B * m + diag[1]
            q = times(wide(left), wide(right))
            qref[g] = wide(q)
            if some is None:
                zref[g] = q
            else:
                some(g)

    def finish(some):
        for g in range(G):
            mref[g] = times(wide(tref[g]), qref[g])
            some(g)

    frob = []
    for g in range(G):
        rows = picked[pl.ds(g * slots, slots), :].astype(bf16)
        value = worth[pl.ds(g * slots, slots), :].astype(bf16)
        both = lax.dot_general(rows, jnp.concatenate([rows, value], axis=1), (((0,), (0,)), ((), ())), preferred_element_type=f32)
        acc[g] = both[:, members:].T[:8]
        system = eye + both[:, :members] * f32(1.0 / 127.0)
        fr = jnp.sqrt(jnp.sum(system * system, axis=(0, 1), keepdims=True))
        frob.append(fr)
        mref[g] = system * (0.5 / fr)
    square(nothing)
    factor(None)
    for g in range(G):
        tref[g] = times(wref[g], qref[g])
    finish(nothing)

    def sweep(k, _):
        square(gather([3 * k, 3 * k + 1, 3 * k + 2], 0))
        factor(gather([3 * k, 3 * k + 1, 3 * k + 2], 1))
        some = gather([3 * k, 3 * k + 1, 3 * k + 2], 2)
        for g in range(G):
            out = times(jnp.concatenate([wref[g], wide(zref[g])], axis=0), qref[g])
            tref[g] = out[:members]
            zref[g] = out[members:]
            some(g)
        finish(gather([3 * k, 3 * k + 1, 3 * k + 2], 3))
        return 0
    lax.fori_loop(0, 0 if 's' in AB else SWEEPS // 2 - 2, sweep, 0)

    square(gather([6, 7], 0))
    factor(gather([6, 7], 1))
    some = gather([6, 7], 2)
    for g in range(G):
        root = times(wide(zref[g]), qref[g]) * (1.0 / jnp.sqrt(frob[g] * f32(127.0)))
        zref[g] = root
        wref[g] = wide(root)
        some(g)
    some = gather([6, 7], 3)
    means = []
    for g in range(G):
        means.append(times(wide(acc[g]), wref[g]))
        some(g)
    for g in range(G):
        means[g] = times(wide(means[g]), wref[g])
    for g in range(G):
        weights_t = (jnp.sqrt(f32(127.0)) * zref[g] + means[g][:1]).astype(bf16)
        patch = step * G + g
        seen = count_ref[patch] > 0
        land = jnp.zeros((8, members), jnp.int32)
        for c in range(8):
            land = jnp.where(column == c, jnp.where(seen, mask_ref[patch, c], 0), land)
        values = state_ref[g].astype(f32)
        center = jnp.sum(values, axis=-1, keepdims=True) * f32(1.0 / members)
        spread = (values - center).astype(bf16)
        got = center + lax.dot_general(spread, weights_t, (((1,), (1,)), ((), ())), preferred_element_type=f32)
        n = values.shape[0]
        res = jnp.where(land[None] > 0, got.reshape(n // 8, 8, members), values.reshape(n // 8, 8, members))
        out_ref[g] = res.reshape(n, members).astype(bf16)

def analyse_patches(idx, vals, counts, mask, tiles, state, G=8, CH=512, AB=''):
    N = state.shape[0]
    slots = idx.size // N
    pool = tiles[0].shape[0]
    rows = state.shape[1]
    return pl.pallas_call(
        functools.partial(body, G, CH, AB),
        grid_spec=pltpu.PrefetchScalarGridSpec(
            num_scalar_prefetch=2,
            grid=(N // G,),
            in_specs=[pl.BlockSpec(memory_space=pl.ANY)] * 11 + [
                pl.BlockSpec((G, rows, 128), lambda i, *s: (i, 0, 0)),
            ],
            out_specs=pl.BlockSpec((G, rows, 128), lambda i, *s: (i, 0, 0)),
            scratch_shapes=[
                pltpu.SMEM(idx.shape, jnp.int32),
                pltpu.SMEM(vals.shape, f32),
                pltpu.VMEM((9 * pool + 8, 128), f32),
                pltpu.VMEM((G * slots, 128), f32),
                pltpu.VMEM((G * slots, 128), f32),
                pltpu.VMEM((2, 128, 128), f32),
                pltpu.VMEM((9, pool, 128), bf16),
                pltpu.VMEM((G, 8, 128), f32),
                pltpu.VMEM((G, 128, 128), f32),
                pltpu.VMEM((G, 128, 128), f32),
                pltpu.VMEM((G, 128, 128), f32),
                pltpu.VMEM((G, 128, 256), bf16),
                pltpu.VMEM((G, 128, 256), bf16),
                pltpu.SemaphoreType.DMA((9,)),
                pltpu.SemaphoreType.DMA((2,)),
            ],
        ),
        out_shape=jax.ShapeDtypeStruct(state.shape, bf16),
        compiler_params=pltpu.CompilerParams(vmem_limit_bytes=56 * 1024 * 1024, dimension_semantics=("arbitrary",)),
        cost_estimate=pl.CostEstimate(flops=int(64*1.2e9), bytes_accessed=24_000_000, transcendentals=0),
        name="analyse_patches",
    )(counts, mask, idx, vals, *tiles, state)


MESH = pl.DeviceIdType.MESH
PIECES = 4
ASIDE = 1


def halo_body(lats, lons, pert, innov, prec, picks, counts, *refs):
    outs = refs[:8]
    own_out, vals, places = refs[8:11]
    own, own_vals, zeros, row_send, row_recv, val_send, val_recv, side_send, local = refs[11:]
    a, b = lax.axis_index("lat"), lax.axis_index("lon")
    pool, members = own.shape
    size = pool // PIECES
    lines = pool // members
    slots = {}
    for u in range(3):
        for v in range(3):
            if (u, v) != (1, 1):
                slots[u, v] = outs[len(slots)]

    def at(u, v):
        return (a + u, lax.rem(b + v + lons, lons))

    def rows(u, v, source, target, piece, number, send=None):
        return pltpu.make_async_remote_copy(
            src_ref=source.at[pl.ds(piece * size, size)],
            dst_ref=slots[target].at[pl.ds(piece * size, size)],
            send_sem=row_send.at[number, piece] if send is None else side_send.at[send, piece],
            recv_sem=row_recv.at[number, piece],
            device_id=at(u, v),
            device_id_type=MESH,
        )

    def place(u, v):
        return vals.at[pl.ds((3 * u + v) * lines, lines)]

    def numbers(u, v, source, target, number):
        return pltpu.make_async_remote_copy(
            src_ref=source,
            dst_ref=place(*target),
            send_sem=val_send.at[number],
            recv_sem=val_recv.at[number],
            device_id=at(u, v),
            device_id_type=MESH,
        )

    has_up, has_down = a > 0, a < lats - 1
    even = lax.rem(a, 2) == 0
    barrier = pltpu.get_barrier_semaphore()
    for v in (-1, 1):
        pl.semaphore_signal(barrier, inc=1, device_id=at(0, v), device_id_type=MESH)

    @pl.when(has_up)
    def _():
        pl.semaphore_signal(barrier, inc=1, device_id=at(-1, 0), device_id_type=MESH)

    @pl.when(has_down)
    def _():
        pl.semaphore_signal(barrier, inc=1, device_id=at(1, 0), device_id_type=MESH)

    across = [[rows(0, 1, own, (1, 0), p, 0) for p in range(PIECES)], [rows(0, -1, own, (1, 2), p, 1) for p in range(PIECES)]]
    across_vals = [numbers(0, 1, own_vals, (1, 0), 0), numbers(0, -1, own_vals, (1, 2), 1)]
    source = [slots[1, 0], own, slots[1, 2]]
    source_vals = [place(1, 0), own_vals, place(1, 2)]
    down = [[rows(1, 0, source[w], (0, w), p, 2 + 2 * w) for p in range(PIECES)] for w in range(3)]
    up = [[rows(-1, 0, source[w], (2, w), p, 3 + 2 * w) for p in range(PIECES)] for w in range(3)]
    down_vals = [numbers(1, 0, source_vals[w], (0, w), 2 + 2 * w) for w in range(3)]
    up_vals = [numbers(-1, 0, source_vals[w], (2, w), 3 + 2 * w) for w in range(3)]
    last = range(PIECES - ASIDE, PIECES)
    side_up = [rows(0, 1, slots[0, 1], (0, 0), p, 2, 0) for p in last] + [rows(0, -1, slots[0, 1], (0, 2), p, 6, 1) for p in last]
    side_down = [rows(0, 1, slots[2, 1], (2, 0), p, 3, 0) for p in last] + [rows(0, -1, slots[2, 1], (2, 2), p, 7, 1) for p in last]

    def onward(copies_down, copies_up, aside=False):
        @pl.when(has_down & even if aside else has_down)
        def _():
            for copy in copies_down:
                copy.start()

        @pl.when(has_up & jnp.logical_not(even) if aside else has_up)
        def _():
            for copy in copies_up:
                copy.start()

    root = jnp.sqrt(prec[...])
    own_vals[...] = (root * innov[...]).astype(bf16).astype(f32)
    zeros[...] = jnp.zeros_like(zeros)
    turned = jnp.concatenate([root] * (members // lines), axis=0).T
    for p in range(PIECES):
        for r in range(p * lines // PIECES, (p + 1) * lines // PIECES):
            here = pl.ds(r * members, members)
            own[here, :] = (turned[:, r : r + 1] * pert[here, :].astype(f32)).astype(bf16)
        if p == 0:
            pl.semaphore_wait(barrier, 2 + jnp.minimum(a, 1) + jnp.minimum(lats - 1 - a, 1))
        across[0][p].start()
        across[1][p].start()
        onward([down[1][p]], [up[1][p]])
        if p == 0:
            for copy in across_vals:
                copy.start()
            onward([down_vals[1]], [up_vals[1]])
    keep = [
        pltpu.make_async_copy(own, own_out, local.at[0]),
        pltpu.make_async_copy(own_vals, place(1, 1), local.at[1]),
        pltpu.make_async_copy(zeros, vals.at[pl.ds(9 * lines, zeros.shape[0])], local.at[2]),
    ]
    for copy in keep:
        copy.start()

    patches = counts.shape[1]
    line = lax.broadcasted_iota(jnp.int32, (patches, patches), 0)
    same = line == lax.broadcasted_iota(jnp.int32, (patches, patches), 1)
    spread_counts = jnp.broadcast_to(counts[...].astype(f32), (patches, patches))
    limit = jnp.sum(jnp.where(same, spread_counts, 0.0), axis=1, keepdims=True)
    slot = lax.broadcasted_iota(jnp.int32, (patches, members), 1).astype(f32)
    for h in range(picks.shape[1] // members):
        seen = slot + h * members < limit
        places[pl.ds(h * patches, patches), :] = jnp.where(seen, picks[:, h * members : (h + 1) * members], 9 * pool)

    across_vals[0].wait_recv()
    onward([down_vals[0]], [up_vals[0]])
    across_vals[1].wait_recv()
    onward([down_vals[2]], [up_vals[2]])
    for p in range(PIECES):
        if p == PIECES - ASIDE:

            @pl.when(even & has_up)
            def _():
                for q in last:
                    down[1][q].wait_recv()
                for copy in side_up:
                    copy.start()

            @pl.when(jnp.logical_not(even) & has_down)
            def _():
                for q in last:
                    up[1][q].wait_recv()
                for copy in side_down:
                    copy.start()

        for d in range(2):
            across[d][p].wait_recv()
            onward([down[2 * d][p]], [up[2 * d][p]], p in last)

    for copy in keep:
        copy.wait()
    for copy in across_vals + across[0] + across[1]:
        copy.wait_send()

    def corners(copies, pieces):
        return [copies[w][p] for w in (0, 2) for p in pieces]

    first = range(PIECES - ASIDE)

    @pl.when(has_down)
    def _():
        for copy in down_vals + down[1] + corners(down, first):
            copy.wait_send()
        for copy in up_vals + up[1][: PIECES - ASIDE] + corners(up, range(PIECES)):
            copy.wait_recv()

    @pl.when(has_up)
    def _():
        for copy in up_vals + up[1] + corners(up, first):
            copy.wait_send()
        for copy in down_vals + down[1][: PIECES - ASIDE] + corners(down, range(PIECES)):
            copy.wait_recv()

    @pl.when(has_down & even)
    def _():
        for copy in corners(down, last):
            copy.wait_send()
        for copy in up[1][PIECES - ASIDE :]:
            copy.wait_recv()

    @pl.when(has_up & jnp.logical_not(even))
    def _():
        for copy in corners(up, last):
            copy.wait_send()
        for copy in down[1][PIECES - ASIDE :]:
            copy.wait_recv()

    @pl.when(has_up & even)
    def _():
        for copy in side_up:
            copy.wait_send()

    @pl.when(has_down & jnp.logical_not(even))
    def _():
        for copy in side_down:
            copy.wait_send()


def halo(pert, innov, prec, picks, counts):
    lats, lons = lax.axis_size("lat"), lax.axis_size("lon")
    pool, members = pert.shape
    lines = pool // members
    vmem = pl.BlockSpec(memory_space=pltpu.VMEM)
    anywhere = pl.BlockSpec(memory_space=pl.ANY)
    got = pl.pallas_call(
        functools.partial(halo_body, lats, lons),
        in_specs=[vmem] * 5,
        out_specs=[anywhere] * 10 + [vmem],
        out_shape=[jax.ShapeDtypeStruct((pool, members), bf16)] * 9
        + [
            jax.ShapeDtypeStruct((9 * lines + 8, members), f32),
            jax.ShapeDtypeStruct((picks.size // members, members), jnp.int32),
        ],
        scratch_shapes=[
            pltpu.VMEM((pool, members), bf16),
            pltpu.VMEM((lines, members), f32),
            pltpu.VMEM((8, members), f32),
            pltpu.SemaphoreType.DMA((8, PIECES)),
            pltpu.SemaphoreType.DMA((8, PIECES)),
            pltpu.SemaphoreType.DMA((8,)),
            pltpu.SemaphoreType.DMA((8,)),
            pltpu.SemaphoreType.DMA((2, PIECES)),
            pltpu.SemaphoreType.DMA((3,)),
        ],
        compiler_params=pltpu.CompilerParams(collective_id=0, has_side_effects=True),
        name="halo",
    )(pert, innov, prec, picks, counts)
    return list(got[:4]) + [got[8]] + list(got[4:8]), got[9], got[10]


def shards(state, ocean_mask, obs_pert, innovation, precision, obs_index, obs_count):
    pool, members = obs_pert.shape[2:]
    patches = obs_index.shape[2]
    lines = (pool // members, members)
    tiles, vals, places = halo(
        obs_pert[0, 0], innovation.reshape(lines), precision.reshape(lines), obs_index[0, 0], obs_count[0]
    )
    columns = state.reshape(patches, -1, members)
    out = analyse_patches(places, vals.reshape(-1), obs_count[0, 0], ocean_mask[0, 0], tiles, columns)
    return out.reshape(state.shape)


def solution(mesh):
    placed = (
        P("lat", "lon", None, None, None, None),
        P("lat", "lon", None, None),
        P("lat", "lon", None, None),
        P("lat", "lon", None),
        P("lat", "lon", None),
        P("lat", "lon", None, None),
        P("lat", "lon", None),
    )
    return jax.shard_map(
        shards,
        mesh=mesh,
        in_specs=placed,
        out_specs=P("lat", "lon", None, None, None, None),
        check_vma=False,
    )
```

time: 120 us -> 99 us (0.82)
  Pallas kernels: 110 us -> 97.3 us
  other arithmetic: 5.94 us -> 0 us
  local copies, waits for them, and re-layouts: 4 us -> 1.38 us
    pallas_call x1, Pallas kernels: 64 us -> 55.4 us  [analyse_patches(): pl.pallas_call(functools.partial(body, G, CH, AB), grid_spec=pltpu.Prefet...]
    convert_element_type x3 -> x0, other arithmetic: 4.56 us -> none  [the longest x1 2.54 us: shards(): scaled = (root_prec[:, None] * obs_pert[0, 0].astype(f32)).astype(bf16)]
    pallas_call x1, Pallas kernels: 45.8 us -> 41.9 us  [halo(): pl.pallas_call(functools.partial(halo_body, lats, lons), in_specs=[vmem]...]
    broadcast_in_dim x2 -> x0, local copies, waits for them, and re-layouts: 1.43 us -> none  [the longest x1 0.84 us: shards(): updated = jnp.broadcast_to(updated[:, :, None], updated.shape + (members,))]
    unnamed x0 -> x1, local copies, waits for them, and re-layouts: none -> 1.38 us
where the time goes in v3:
time: 99 us; the launch traced here: 98.7 us
  Pallas kernels  97.3 us (98%)
  local copies, waits for them, and re-layouts  1.38 us (1%)
    pallas_call x1, Pallas kernels, analyse_patches(): pl.pallas_call(functools.partial(body, G, CH, AB), grid_spec=pltpu.Prefet...  55.4 us
    pallas_call x1, Pallas kernels, halo(): pl.pallas_call(functools.partial(halo_body, lats, lons), in_specs=[vmem]...  41.9 us

profile of v3, /device:TPU:1, one launch (start us, length us, event | category | flops | bytes accessed | tf_op | source)
XLA Modules:
  0.0 98.7 jit_solution(1207735375736925602)
XLA Ops:
  0.0 1.4 %copy.8 = s32[1,1,64,8]{3,2,1,0:T(8,128)} copy(s32[1,1,64,8]{2,3,1,0:T(8,128)} %param.8) | data formatting | bytes 4096 | tf_op args[1]
  1.4 41.9 %halo.1 = (bf16[4096,128]{1,0:T(8,128)(2,1)}, bf16[4096,128]{1,0:T(8,128)(2,1)}, bf16[4096,128]{1,0:T(8,128)(2,1)}, bf16[4096,128]{1,0:T(8,128)(2,1)}, bf16[4096...) custom-call(bf16[4096,128]{1,0:T(8,128)(2,1)} %bitcast.10, ...), custom_call_target="tpu_custom_call" | custom-call | tf_op jit(solution)/shard_map/halo/pallas_call | solution.py:410
  43.3 55.4 %analyse_patches.1 = bf16[64,400,128]{2,1,0:T(8,128)(2,1)} custom-call(s32[64]{0:T(128)} %bitcast.16, s32[64,8]{1,0:T(8,128)} %bitcast.12, s32[128,128]{1,0:T(8,128)} %get-tuple-element.16.idx_hbm, f32[37888]{0:T(1024)} %bitcast.18, bf16[4096,128]{1,0:T(8,128)(2,1)} %get-tuple-element.18.refs_0_, bf16[4096,128]{1,0:T(8,128)(2,1)} %get-tuple-element.19.refs_1_, ...), custom_call_target="tpu_custom_call" | custom-call | flops 76800000000 | bytes 24000000 | tf_op jit(solution)/shard_map/analyse_patches/pallas_call | solution.py:179

commit v4 on v3

--- a/solution.py
+++ b/solution.py
@@ -32,13 +32,17 @@
     patches = steps * G
     pool = tiles[0].shape[0]
 
-    def pick(group, g, start, count):
-        p = group * G + g
-        base = pl.multiple_of(g * slots, slots)
+    def pick(g, start, count):
         for u in range(start, start + count):
-            i = idx_ref[p + u // lanes * patches, u % lanes]
-            picked[pl.ds(base + u, 1), :] = table[pl.ds(i, 1), :]
-            worth[pl.ds(base + u, 1), :] = jnp.full((1, members), val_ref[i], f32)
+            i = idx_ref[g + u // lanes * G, u % lanes]
+            picked[pl.ds(g * slots + u, 1), :] = table[pl.ds(i, 1), :]
+            worth[pl.ds(g * slots + u, 1), :] = jnp.full((1, members), val_ref[i], f32)
+
+    def list_of(group):
+        return [
+            pltpu.make_async_copy(idx_hbm.at[pl.ds(h * patches + group * G, G)], idx_ref.at[pl.ds(h * G, G)], smem_sem.at[h])
+            for h in range(slots // lanes)
+        ]
 
     rows_i = lax.broadcasted_iota(jnp.int32, (members, members), 0)
     cols_i = lax.broadcasted_iota(jnp.int32, (members, members), 1)
@@ -49,7 +53,7 @@
 
     @pl.when(step == (-1 if 't' in AB else 0))
     def _():
-        scalars = [pltpu.make_async_copy(idx_hbm, idx_ref, smem_sem.at[0]), pltpu.make_async_copy(val_hbm, val_ref, smem_sem.at[1])]
+        scalars = list_of(0) + [pltpu.make_async_copy(val_hbm, val_ref, smem_sem.at[slots // lanes])]
         for copy in scalars:
             copy.start()
         for t in range(9):
@@ -69,12 +73,12 @@
         for j in range(2):
             diag[j] = eye * (SHIFT_A, SHIFT_B)[j]
 
-        def first(g, _):
-            pick(0, g, 0, slots)
-            return 0
-        lax.fori_loop(0, G, first, 0)
-
-    group = jnp.minimum(step + 1, steps - 1)
+        for g in range(G):
+            pick(g, 0, slots)
+
+    following = list_of(jnp.minimum(step + 1, steps - 1))
+    for copy in following:
+        copy.start()
 
     column = lax.broadcasted_iota(jnp.int32, (8, members), 0)
 
@@ -82,7 +86,7 @@
         count = len(patches) * slots // 4 // G
         def some(g):
             for u in range((stage_no * G + g) * count, (stage_no * G + g + 1) * count, 8):
-                pick(group, patches[u // slots], u % slots, 8)
+                pick(patches[u // slots], u % slots, 8)
         return some
 
     def nothing(g):
@@ -114,11 +118,12 @@
 
     frob = []
     for g in range(G):
-        rows = picked[pl.ds(g * slots, slots), :].astype(bf16)
-        value = worth[pl.ds(g * slots, slots), :].astype(bf16)
-        both = lax.dot_general(rows, jnp.concatenate([rows, value], axis=1), (((0,), (0,)), ((), ())), preferred_element_type=f32)
-        acc[g] = both[:, members:].T[:8]
-        system = eye + both[:, :members] * f32(1.0 / 127.0)
+        chosen = picked[pl.ds(g * slots, slots), :]
+        product = (chosen * worth[pl.ds(g * slots, slots), :]).reshape(slots // 8, 8, members)
+        acc[g] = jnp.broadcast_to(jnp.sum(jnp.sum(product, axis=0), axis=0, keepdims=True), (8, members))
+        rows = chosen.astype(bf16)
+        gram = lax.dot_general(rows, rows, (((0,), (0,)), ((), ())), preferred_element_type=f32)
+        system = eye + gram * f32(1.0 / 127.0)
         fr = jnp.sqrt(jnp.sum(system * system, axis=(0, 1), keepdims=True))
         frob.append(fr)
         mref[g] = system * (0.5 / fr)
@@ -128,19 +133,22 @@
         tref[g] = times(wref[g], qref[g])
     finish(nothing)
 
-    def sweep(k, _):
-        square(gather([3 * k, 3 * k + 1, 3 * k + 2], 0))
-        factor(gather([3 * k, 3 * k + 1, 3 * k + 2], 1))
-        some = gather([3 * k, 3 * k + 1, 3 * k + 2], 2)
+    for copy in following:
+        copy.wait()
+
+    def sweep(chosen):
+        square(gather(chosen, 0))
+        factor(gather(chosen, 1))
+        some = gather(chosen, 2)
         for g in range(G):
             out = times(jnp.concatenate([wref[g], wide(zref[g])], axis=0), qref[g])
             tref[g] = out[:members]
             zref[g] = out[members:]
             some(g)
-        finish(gather([3 * k, 3 * k + 1, 3 * k + 2], 3))
-        return 0
-    lax.fori_loop(0, 0 if 's' in AB else SWEEPS // 2 - 2, sweep, 0)
-
+        finish(gather(chosen, 3))
+
+    sweep([0, 1, 2])
+    sweep([3, 4, 5])
     square(gather([6, 7], 0))
     factor(gather([6, 7], 1))
     some = gather([6, 7], 2)
@@ -186,7 +194,7 @@
             ],
             out_specs=pl.BlockSpec((G, rows, 128), lambda i, *s: (i, 0, 0)),
             scratch_shapes=[
-                pltpu.SMEM(idx.shape, jnp.int32),
+                pltpu.SMEM((G * slots // 128, 128), jnp.int32),
                 pltpu.SMEM(vals.shape, f32),
                 pltpu.VMEM((9 * pool + 8, 128), f32),
                 pltpu.VMEM((G * slots, 128), f32),
@@ -200,7 +208,7 @@
                 pltpu.VMEM((G, 128, 256), bf16),
                 pltpu.VMEM((G, 128, 256), bf16),
                 pltpu.SemaphoreType.DMA((9,)),
-                pltpu.SemaphoreType.DMA((2,)),
+                pltpu.SemaphoreType.DMA((slots // 128 + 1,)),
             ],
         ),
         out_shape=jax.ShapeDtypeStruct(state.shape, bf16),

time: 99 us -> 96.8 us (0.978)
  Pallas kernels: 97.3 us -> 95.2 us
    pallas_call x1, Pallas kernels: 55.4 us -> 53.3 us  [analyse_patches(): pl.pallas_call(functools.partial(body, G, CH, AB), grid_spec=pltpu.Prefet...]
where the time goes in v4:
time: 96.8 us; the launch traced here: 96.6 us
  Pallas kernels  95.2 us (98%)
  local copies, waits for them, and re-layouts  1.38 us (1%)
    pallas_call x1, Pallas kernels, analyse_patches(): pl.pallas_call(functools.partial(body, G, CH, AB), grid_spec=pltpu.Prefet...  53.3 us
    pallas_call x1, Pallas kernels, halo(): pl.pallas_call(functools.partial(halo_body, lats, lons), in_specs=[vmem]...  41.9 us

profile of v4, /device:TPU:1, one launch (start us, length us, event | category | flops | bytes accessed | tf_op | source)
XLA Modules:
  0.0 96.6 jit_solution(3240595194105754530)
XLA Ops:
  0.0 1.4 %copy.8 = s32[1,1,64,8]{3,2,1,0:T(8,128)} copy(s32[1,1,64,8]{2,3,1,0:T(8,128)} %param.8) | data formatting | bytes 4096 | tf_op args[1]
  1.4 41.9 %halo.1 = (bf16[4096,128]{1,0:T(8,128)(2,1)}, bf16[4096,128]{1,0:T(8,128)(2,1)}, bf16[4096,128]{1,0:T(8,128)(2,1)}, bf16[4096,128]{1,0:T(8,128)(2,1)}, bf16[4096...) custom-call(bf16[4096,128]{1,0:T(8,128)(2,1)} %bitcast.10, ...), custom_call_target="tpu_custom_call" | custom-call | tf_op jit(solution)/shard_map/halo/pallas_call | solution.py:418
  43.3 53.3 %analyse_patches.1 = bf16[64,400,128]{2,1,0:T(8,128)(2,1)} custom-call(s32[64]{0:T(128)} %bitcast.16, s32[64,8]{1,0:T(8,128)} %bitcast.12, s32[128,128]{1,0:T(8,128)} %get-tuple-element.16.idx_hbm, f32[37888]{0:T(1024)} %bitcast.18, bf16[4096,128]{1,0:T(8,128)(2,1)} %get-tuple-element.18.refs_0_, bf16[4096,128]{1,0:T(8,128)(2,1)} %get-tuple-element.19.refs_1_, ...), custom_call_target="tpu_custom_call" | custom-call | flops 76800000000 | bytes 24000000 | tf_op jit(solution)/shard_map/analyse_patches/pallas_call | solution.py:187
